TPU v7x, 32 devices: a whole 2x2x4 slice. The times are simulated.
32 devices in a mesh: acq: 4 (over x, core), pulse: 8 (over z, y).
Axes of the slice: x: 2, y: 2, z: 4, core: 2. Of those that a mesh axis runs over, the one named last changes fastest.
Arguments:
- raw_echo: bfloat16 [4, 2, 8192, 1535], P('acq', None, 'pulse'), may hold values from -6 to 6
- chirp_phase: float32 [1024], replicated, may hold values from -3.140625 to 3.140625
- pulse_counts: int32 [4], P('acq'), may hold values from 4096 to 8192, as said below
- azimuth_rate: float32 [512], P('pulse'), may hold values from 0.25 to 1
- partner_bits: int32 [4, 2], P('acq'), may hold values from 0 to 1, as said below
Outputs:
- interfere_real: float32 [4, 2, 128, 512], P('acq', None, 'pulse')
- interfere_imag: float32 [4, 2, 128, 512], P('acq', None, 'pulse')
Inputs may be any that keep to these rules, and one draw needn't show every extreme that they name: `pulse_counts`: at least half of 8192; some acquisition records all 8192 pulses and some exactly half. `partner_bits`: the two bits of a row differ.
All inputs are finite; a program needn't handle non-finite values.
Results may differ from a plain program's by a relative error of at most 0.0065.
Values may be sent and summed in bfloat16 or wider, within the bound.
A program may use at most 64 MiB of HBM per device.

v0:
```python
import math

import jax
import jax.numpy as jnp
from jax import lax
from jax.sharding import PartitionSpec as P

RNG = 512
TAPS = 1024
LOOK_RNG = 4
LOOK_AZ = 16


def partner_2(shard, axis, bit):
    return lax.ppermute(shard, axis, [(i, i ^ 1 << bit) for i in range(lax.axis_size(axis))])


def part_tables(length, inverse):
    steps = jnp.arange(length, dtype=jnp.int32)
    angle = 2.0 * jnp.pi * (steps[:, None] * steps[None, :] % length).astype(jnp.float32) / length
    cosine = jnp.cos(angle)
    sine = jnp.sin(angle)
    if inverse:
        sine = -sine
    return jnp.stack([jnp.stack([cosine, -sine]), jnp.stack([sine, cosine])])


def complex_product(left_re, left_im, right_re, right_im):
    return (left_re * right_re - left_im * right_im, left_re * right_im + left_im * right_re)


def compress(echoes, toeplitz, first_pulse, live_pulses, block_cols, window):
    pulse_rows = echoes.shape[1]
    parts_re = []
    parts_im = []
    for start in range(0, RNG, block_cols):
        segment = echoes[:, :, start : start + window]
        stacked = jnp.concatenate([segment[0], segment[1]], axis=1)
        result = lax.dot_general(
            toeplitz, stacked, (((1,), (1,)), ((), ())), preferred_element_type=jnp.float32
        )
        parts_re.append(result[:block_cols])
        parts_im.append(result[block_cols:])
    joined = jnp.stack([jnp.concatenate(parts_re, axis=0), jnp.concatenate(parts_im, axis=0)])
    pulse_ids = first_pulse + jnp.arange(pulse_rows, dtype=jnp.int32)
    keep = (pulse_ids < live_pulses).astype(jnp.float32)
    return (joined * keep[None, None, :]).astype(jnp.bfloat16)


def azimuth(turned, azimuth_rate):
    columns = turned.shape[1]
    length = turned.shape[2]
    outer_len = 64
    inner_len = length // outer_len
    highest = lax.Precision.HIGHEST
    signal = turned.astype(jnp.float32).reshape(2, columns, outer_len, inner_len)
    section_one = jnp.einsum(
        "pcab,pqak->qckb", signal, part_tables(outer_len, False), precision=highest
    )
    outer_ids = jnp.arange(outer_len, dtype=jnp.int32)
    inner_ids = jnp.arange(inner_len, dtype=jnp.int32)
    twist = (
        2.0
        * jnp.pi
        * (outer_ids[:, None] * inner_ids[None, :] % length).astype(jnp.float32)
        / length
    )
    twist_cos = jnp.cos(twist)
    twist_sin = jnp.sin(twist)
    turned_re, turned_im = complex_product(section_one[0], section_one[1], twist_cos, -twist_sin)
    spectrum = jnp.einsum(
        "pckb,pqbm->qckm",
        jnp.stack([turned_re, turned_im]),
        part_tables(inner_len, False),
        precision=highest,
    )
    freq_index = outer_ids[:, None] + outer_len * inner_ids[None, :]
    signed = jnp.where(freq_index < length // 2, freq_index, freq_index - length).astype(
        jnp.float32
    )
    quad = signed * signed / length
    phase = (jnp.pi * azimuth_rate)[:, None, None] * quad[None, :, :]
    filt_re, filt_im = complex_product(spectrum[0], spectrum[1], jnp.cos(phase), -jnp.sin(phase))
    back_one = jnp.einsum(
        "pckm,pqmb->qckb",
        jnp.stack([filt_re, filt_im]),
        part_tables(inner_len, True),
        precision=highest,
    )
    undo_re, undo_im = complex_product(back_one[0], back_one[1], twist_cos, twist_sin)
    restored = jnp.einsum(
        "pckb,pqka->qcab",
        jnp.stack([undo_re, undo_im]),
        part_tables(outer_len, True),
        precision=highest,
    )
    return (restored / length).reshape(2, columns, length)


def multilook(values):
    columns = values.shape[0]
    pulse_len = values.shape[1]
    shaped = values.reshape(columns // LOOK_RNG, LOOK_RNG, pulse_len // LOOK_AZ, LOOK_AZ)
    return jnp.mean(shaped, axis=(1, 3))


def cross_looks(own_block, partner):
    own_f = own_block.astype(jnp.float32)
    other_f = partner.astype(jnp.float32)
    prod_re = own_f[0] * other_f[0] + own_f[1] * other_f[1]
    prod_im = own_f[1] * other_f[0] - own_f[0] * other_f[1]
    return jnp.stack([multilook(prod_re), multilook(prod_im)])


def per_device(raw_echo, chirp_phase, pulse_counts, azimuth_rate, partner_bits):
    echoes = raw_echo[0]
    pulses_dev = echoes.shape[1]
    block_cols = min(256, RNG)
    window = block_cols + TAPS - 1
    amplitude = 2.0 / math.sqrt(TAPS)
    table_re = (amplitude * jnp.cos(chirp_phase)).astype(jnp.bfloat16)
    table_im = (amplitude * jnp.sin(chirp_phase)).astype(jnp.bfloat16)
    padding = jnp.zeros((block_cols,), jnp.bfloat16)
    band_re = jnp.tile(jnp.concatenate([table_re, padding]), block_cols)[
        : block_cols * window
    ].reshape(block_cols, window)
    band_im = jnp.tile(jnp.concatenate([table_im, padding]), block_cols)[
        : block_cols * window
    ].reshape(block_cols, window)
    toeplitz = jnp.concatenate(
        [jnp.concatenate([band_re, band_im], axis=1), jnp.concatenate([-band_im, band_re], axis=1)],
        axis=0,
    )
    live_pulses = pulse_counts[0]
    first_pulse = lax.axis_index("pulse") * pulses_dev
    compressed = compress(echoes, toeplitz, first_pulse, live_pulses, block_cols, window)
    turned = lax.all_to_all(compressed, "pulse", split_axis=1, concat_axis=2, tiled=True)
    focused = azimuth(turned, azimuth_rate).astype(jnp.bfloat16)
    chosen = partner_bits[0]
    bit_count = lax.axis_size("acq").bit_length() - 1
    arrived = [partner_2(focused, "acq", which) for which in range(bit_count)]
    results = []
    for slot in range(2):
        partner = arrived[0]
        for which in range(1, bit_count):
            partner = jnp.where(chosen[slot] == which, arrived[which], partner)
        results.append(cross_looks(focused, partner))
    interfere_real = jnp.stack([item[0] for item in results])[None]
    interfere_imag = jnp.stack([item[1] for item in results])[None]
    return (interfere_real, interfere_imag)


def solution(mesh):
    in_specs = (P("acq", None, "pulse", None), P(), P("acq"), P("pulse"), P("acq", None))
    out_specs = (P("acq", None, "pulse", None), P("acq", None, "pulse", None))
    return jax.shard_map(
        per_device, mesh=mesh, in_specs=in_specs, out_specs=out_specs, check_vma=False
    )
```

profile of v0, /device:TPU:0, one launch (start us, length us, event | category | flops | bytes accessed | tf_op | source)
XLA Modules:
  0.0 249.3 jit_solution(11335158560890421651)
XLA Ops:
  1.3 0.7 multiply_convert_fusion
  2.1 0.8 tile.9
  2.9 1.2 reshape.360
  4.1 0.8 tile.21
  4.9 1.2 reshape.361
  6.2 16.5 %copy.28 = bf16[1,2,1024,1535]{3,2,1,0:T(8,128)(2,1)} copy(bf16[1,2,1024,1535]{2,1,3,0:T(2,128)(2,1)} %param.5) | data formatting | bytes 12574720 | tf_op args[0]
  22.7 4.6 %slice_bitcast_fusion.3 = (bf16[1024,1279]{1,0:T(8,128)(2,1)S(1)}, bf16[1024,1279]{1,0:T(8,128)(2,1)S(1)}, bf16[1024,1279]{1,0:T(8,128)(2,1)S(1)}, bf16[1024,1279]{1,0:T(8,128)(2,1)S(1)}) fusion(bf16[2,1024,1535]{2,1,0:T(8,128)(2,1)} %bitcast.119), kind=kLoop, calls=%fused_computation.31 | loop fusion | bytes 20955136 | tf_op jit(solution)/shard_map/squeeze | solution.py:38
  27.3 3.0 %fusion.4 = f32[512,1024]{1,0:T(8,128)S(1)} fusion(bf16[1024,1279]{1,0:T(8,128)(2,1)S(1)} %get-tuple-element.7, bf16[1024,1279]{1,0:T(8,128)(2,1)S(1)} %get-tuple-element.8, bf16[256,1279]{1,0:T(8,128)(2,1)S(1)} %reshape.360, bf16[256,1279]{1,0:T(8,128)(2,1)S(1)} %neg.53, bf16[256,1279]{1,0:T(8,128)(2,1)S(1)} %reshape.361), kind=kOutput, calls=%fused_computation.4 | convolution fusion | flops 2703212544 | bytes 9300480 | tf_op jit(solution)/shard_map/dot_general | solution.py:39
  30.3 0.2 fusion.88
  30.5 0.8 copy-done.4
  31.4 3.0 %fusion = f32[512,1024]{1,0:T(8,128)S(1)} fusion(bf16[1024,1279]{1,0:T(8,128)(2,1)S(1)} %get-tuple-element.9, bf16[1024,1279]{1,0:T(8,128)(2,1)S(1)} %get-tuple-element.6, bf16[256,1279]{1,0:T(8,128)(2,1)S(1)} %reshape.360, bf16[256,1279]{1,0:T(8,128)(2,1)S(1)} %copy-done.4, bf16[256,1279]{1,0:T(8,128)(2,1)S(1)} %reshape.361), kind=kOutput, calls=%fused_computation | convolution fusion | flops 2703212544 | bytes 9300480 | tf_op jit(solution)/shard_map/dot_general | solution.py:39
  34.3 1.2 fusion.87
  35.5 1.5 maximum_bitcast_fusion
  37.1 0.6 fusion.8
  37.7 3.5 %copy.29 = bf16[2,512,1024]{2,0,1:T(2,128)(2,1)} copy(bf16[2,512,1024]{2,1,0:T(8,128)(2,1)S(1)} %fusion.8) | data formatting | bytes 4194304 | tf_op jit(solution)/shard_map/convert_element_type | solution.py:47
  41.2 7.6 %all-to-all-start = ((bf16[2,512,1024]{2,0,1:T(2,128)(2,1)}), bf16[2,512,1024]{2,0,1:T(2,128)(2,1)S(1)}, u32[]{:S(2)}, u32[]{:S(2)}) async-start(bf16[2,512,1024]{2,0,1:T(2,128)(2,1)} %copy.29), calls=%async_computation | async-start | bytes 4194304 | tf_op jit(solution)/shard_map/all_to_all | solution.py:137
  48.8 0.1 fusion.80
  49.1 0.3 fusion.75
  49.4 0.1 fusion.78
  49.5 0.1 fusion.77
  49.7 0.3 fusion.69
  50.1 46.9 %all-to-all-done = bf16[2,512,1024]{2,0,1:T(2,128)(2,1)S(1)} async-done(((bf16[2,512,1024]{2,0,1:T(2,128)(2,1)}), bf16[2,512,1024]{2,0,1:T(2,128)(2,1)S(1)}, u32[]{:S(2)}, u32[]{:S(2)}) %all-to-all-start) | async-done | bytes 2097184 | tf_op jit(solution)/shard_map/all_to_all | solution.py:137
  97.0 3.6 %copy.71 = bf16[2,8,64,1024]{3,1,0,2:T(8,128)(2,1)} copy(bf16[2,8,64,1024]{3,0,2,1:T(2,128)(2,1)S(1)} %bitcast.120) | data formatting | bytes 4194304 | tf_op jit(solution)/shard_map/all_to_all | solution.py:137
  100.6 2.8 %reshape.364 = bf16[2,64,64,128,1]{3,2,0,1,4:T(8,128)(2,1)S(1)} reshape(bf16[2,64,8,1024]{3,2,0,1:T(8,128)(2,1)} %bitcast.121) | data formatting | bytes 4194304 | tf_op jit(solution)/shard_map/reshape | solution.py:56
  103.4 1.8 convolution_bitcast_fusion
  105.2 1.0 multiply_subtract_fusion.3
  106.2 3.8 %fusion.22 = f32[2,64,64,128]{3,2,1,0:T(8,128)S(1)} fusion(f32[1,2,128,128]{3,2,0,1:T(8,128)S(1)} %get-tuple-element.25, f32[1,2,128,128]{3,2,0,1:T(8,128)S(1)} %get-tuple-element.32, f32[1,64,64,128]{3,2,1,0:T(8,128)S(1)} %get-tuple-element.13, f32[1,64,64,128]{3,2,1,0:T(8,128)S(1)} %get-tuple-element.12), kind=kOutput, calls=%fused_computation.35 | convolution fusion | flops 3222339584 | bytes 8650752 | tf_op jit(solution)/shard_map/pckb,pqbm->qckm/dot_general | solution.py:71
  110.0 8.5 %fusion.28 = (f32[1,64,64,128]{3,2,1,0:T(8,128)S(1)}, f32[1,64,64,128]{3,2,1,0:T(8,128)S(1)}) fusion(f32[2,64,64,128]{3,2,1,0:T(8,128)S(1)} %fusion.22, f32[64,128]{1,0:T(8,128)S(1)} %fusion.66, f32[64]{0:T(128)S(1)} %broadcast_multiply_fusion), kind=kLoop, calls=%fused_computation.38 | loop fusion | flops 4194304 | bytes 8421632 | tf_op jit(solution)/shard_map/sub | solution.py:29
  118.5 3.4 %fusion.25 = f32[2,64,64,128]{3,2,1,0:T(8,128)S(1)} fusion(f32[1,64,64,128]{3,2,1,0:T(8,128)S(1)} %get-tuple-element.15, f32[1,64,64,128]{3,2,1,0:T(8,128)S(1)} %get-tuple-element.14, f32[1,2,128,128]{3,2,1,0:T(8,128)S(1)} %get-tuple-element.33, f32[1,2,128,128]{3,2,1,0:T(8,128)S(1)} %get-tuple-element.24), kind=kOutput, calls=%fused_computation.36 | convolution fusion | flops 3222339584 | bytes 8650752 | tf_op jit(solution)/shard_map/pckm,pqmb->qckb/dot_general | solution.py:84
  121.9 1.0 multiply_subtract_fusion.2
  122.9 4.1 %fusion.33 = bf16[2,64,64,128]{3,2,1,0:T(8,128)(2,1)S(1)} fusion(f32[1,64,64,128]{3,2,1,0:T(8,128)S(1)} %get-tuple-element.11, f32[1,64,64,128]{3,2,1,0:T(8,128)S(1)} %get-tuple-element.10, f32[1,2,64,64]{2,3,1,0:T(8,128)S(1)} %get-tuple-element.35, f32[1,2,64,64]{2,3,1,0:T(8,128)S(1)} %get-tuple-element.28), kind=kOutput, calls=%fused_computation.43 | convolution fusion | flops 1613774848 | bytes 6356992 | tf_op jit(solution)/shard_map/pckb,pqka->qcab/dot_general | solution.py:91
  127.0 2.3 convert_element_type.148
  129.3 1.5 collective-permute-start
  130.8 0.6 fusion.89
  132.7 2.0 convert_element_type.149
  134.7 42.8 %collective-permute-done = bf16[2,64,8192]{2,1,0:T(8,128)(2,1)S(1)} collective-permute-done((bf16[2,64,8192]{2,1,0:T(8,128)(2,1)}, bf16[2,64,8192]{2,1,0:T(8,128)(2,1)S(1)}, u32[]{:S(2)}, u32[]{:S(2)}) %collective-permute-start) | collective-permute-done | bytes 2097184 | tf_op jit(solution)/shard_map/ppermute | solution.py:15
  177.6 0.5 select_convert_fusion.1
  178.1 3.9 %multiply_subtract_fusion.1 = (f32[1,64,8192]{2,1,0:T(8,128)}, f32[1,64,8192]{2,1,0:T(8,128)}, f32[1,64,8192]{2,1,0:T(8,128)}, f32[1,64,8192]{2,1,0:T(8,128)}) fusion(f32[2,64,8192]{2,1,0:T(8,128)S(1)} %get-tuple-element.18, f32[2,64,8192]{2,1,0:T(8,128)S(1)} %convert_element_type.149, f32[2,64,8192]{2,1,0:T(8,128)S(1)} %get-tuple-element.19), kind=kLoop, calls=%fused_computation.48 | loop fusion | flops 6291456 | bytes 20971520 | tf_op jit(solution)/shard_map/sub | solution.py:111
  182.0 10.3 %sub.43 = f32[16,4,512,16]{3,2,1,0:T(8,128)} reshape(f32[1,64,8192]{2,1,0:T(8,128)} %get-tuple-element.2) | data formatting | bytes 4194304 | tf_op jit(solution)/shard_map/sub | solution.py:111
  192.4 7.1 %reduce_sum.38 = f32[16,512]{1,0:T(8,128)S(1)} reduce(f32[16,4,512,16]{3,2,1,0:T(8,128)} %sub.43, f32[]{:T(128)} %constant.96.clone.1), dimensions={1,3}, to_apply=%region_2.3 | reduce | flops 516096 | bytes 2129924 | tf_op jit(solution)/shard_map/reduce_sum | solution.py:104
  199.5 9.1 %add.185 = f32[16,4,512,16]{3,2,1,0:T(8,128)} reshape(f32[1,64,8192]{2,1,0:T(8,128)S(1)} %copy-done.2) | data formatting | bytes 4194304 | tf_op jit(solution)/shard_map/add | solution.py:110
  208.6 7.1 %reduce_sum.36 = f32[16,512]{1,0:T(8,128)S(1)} reduce(f32[16,4,512,16]{3,2,1,0:T(8,128)} %add.185, f32[]{:T(128)} %constant.96.clone.1), dimensions={1,3}, to_apply=%region_0.1 | reduce | flops 516096 | bytes 2129924 | tf_op jit(solution)/shard_map/reduce_sum | solution.py:104
  215.8 9.0 %add.187 = f32[16,4,512,16]{3,2,1,0:T(8,128)} reshape(f32[1,64,8192]{2,1,0:T(8,128)S(1)} %copy-done.1) | data formatting | bytes 4194304 | tf_op jit(solution)/shard_map/add | solution.py:110
  224.8 7.1 %reduce_sum.37 = f32[16,512]{1,0:T(8,128)S(1)} reduce(f32[16,4,512,16]{3,2,1,0:T(8,128)} %add.187, f32[]{:T(128)} %constant.96.clone.1), dimensions={1,3}, to_apply=%region_1.2 | reduce | flops 516096 | bytes 2129924 | tf_op jit(solution)/shard_map/reduce_sum | solution.py:104
  231.9 9.0 %sub.45 = f32[16,4,512,16]{3,2,1,0:T(8,128)} reshape(f32[1,64,8192]{2,1,0:T(8,128)S(1)} %copy-done) | data formatting | bytes 4194304 | tf_op jit(solution)/shard_map/sub | solution.py:111
  240.9 7.0 %reduce_sum.39 = f32[16,512]{1,0:T(8,128)S(1)} reduce(f32[16,4,512,16]{3,2,1,0:T(8,128)} %sub.45, f32[]{:T(128)} %constant.96.clone.1), dimensions={1,3}, to_apply=%region_3.4 | reduce | flops 516096 | bytes 2129924 | tf_op jit(solution)/shard_map/reduce_sum | solution.py:104
  247.9 0.6 maximum_bitcast_fusion.8
  248.5 0.6 maximum_bitcast_fusion.9
  (31 shorter events, 0.5 us)
Async XLA Ops:
  6.2 21.1 %copy-start.3 = (bf16[256,1279]{1,0:T(8,128)(2,1)}, bf16[256,1279]{1,0:T(8,128)(2,1)S(1)}, u32[]{:S(2)}) copy-start(bf16[256,1279]{1,0:T(8,128)(2,1)S(1)} %neg.53) | copy-start | bytes 1964548
  30.3 1.1 copy-start.4
  41.2 8.9 %copy-start.6 = (f32[64]{0:T(128)S(1)}, f32[64]{0:T(128)}, u32[]{:S(2)}) copy-start(f32[64]{0:T(128)} %param.8) | copy-start | bytes 772
  41.2 55.8 %all-to-all-start = ((bf16[2,512,1024]{2,0,1:T(2,128)(2,1)}), bf16[2,512,1024]{2,0,1:T(2,128)(2,1)S(1)}, u32[]{:S(2)}, u32[]{:S(2)}) async-start(bf16[2,512,1024]{2,0,1:T(2,128)(2,1)} %copy.29), calls=%async_computation | async-start | bytes 4194304 | tf_op jit(solution)/shard_map/all_to_all | solution.py:137
  127.0 3.8 %copy-start.5 = (s32[1,2]{1,0:T(1,128)S(1)}, s32[1,2]{1,0:T(1,128)}, u32[]{:S(2)}) copy-start(s32[1,2]{1,0:T(1,128)} %param.9) | copy-start | bytes 28
  129.3 5.4 %collective-permute-start.1 = (bf16[2,64,8192]{2,1,0:T(8,128)(2,1)}, bf16[2,64,8192]{2,1,0:T(8,128)(2,1)S(1)}, u32[]{:S(2)}, u32[]{:S(2)}) collective-permute-start(bf16[2,64,8192]{2,1,0:T(8,128)(2,1)} %convert_element_type.148), channel_id=1, source_target_pairs={{0,8},{8,0},{16,24},{24,16},{1,9},{9,1},{17,25},{25,17},{2,10},{10... | collective-permute-start | bytes 6291464 | tf_op jit(solution)/shard_map/ppermute | solution.py:15
  129.3 48.3 %collective-permute-start = (bf16[2,64,8192]{2,1,0:T(8,128)(2,1)}, bf16[2,64,8192]{2,1,0:T(8,128)(2,1)S(1)}, u32[]{:S(2)}, u32[]{:S(2)}) collective-permute-start(bf16[2,64,8192]{2,1,0:T(8,128)(2,1)} %convert_element_type.148), channel_id=1, source_target_pairs={{0,16},{8,24},{16,0},{24,8},{1,17},{9,25},{17,1},{25,9},{2,18},{10... | collective-permute-start | bytes 6291464 | tf_op jit(solution)/shard_map/ppermute | solution.py:15
  192.4 7.1 %copy-start.2 = (f32[1,64,8192]{2,1,0:T(8,128)S(1)}, f32[1,64,8192]{2,1,0:T(8,128)}, u32[]{:S(2)}) copy-start(f32[1,64,8192]{2,1,0:T(8,128)} %get-tuple-element.3) | copy-start | bytes 6291460
  208.6 7.2 %copy-start.1 = (f32[1,64,8192]{2,1,0:T(8,128)S(1)}, f32[1,64,8192]{2,1,0:T(8,128)}, u32[]{:S(2)}) copy-start(f32[1,64,8192]{2,1,0:T(8,128)} %get-tuple-element.16) | copy-start | bytes 6291460
  224.8 7.1 %copy-start = (f32[1,64,8192]{2,1,0:T(8,128)S(1)}, f32[1,64,8192]{2,1,0:T(8,128)}, u32[]{:S(2)}) copy-start(f32[1,64,8192]{2,1,0:T(8,128)} %get-tuple-element.17) | copy-start | bytes 6291460
where the time goes:
time: 254 us; the launch traced here: 249 us
  waiting for transfers between devices  89.8 us (35%)
  local copies, waits for them, and re-layouts  77.5 us (31%)
  other arithmetic  50.7 us (20%)
  matrix products  19.1 us (8%)
  starting transfers between devices  9.15 us (4%)
  between operations  3.14 us (1%)
    all_to_all x1, waiting for transfers between devices, per_device(): lax.all_to_all(compressed, 'pulse', split_axis=1, concat_axis=2, tiled=True)  46.9 us
    ppermute x2, waiting for transfers between devices, partner_2(): lax.ppermute(shard, axis, [(i, i ^ 1 << bit) for i in range(lax.axis_size...  42.8 us
    reduce_sum x4, other arithmetic, multilook(): return jnp.mean(shaped, axis=(1, 3))  28.4 us
    sub x2, local copies, waits for them, and re-layouts, cross_looks(): prod_im = own_f[1] * other_f[0] - own_f[0] * other_f[1]  19.3 us
    add x2, local copies, waits for them, and re-layouts, cross_looks(): prod_re = own_f[0] * other_f[0] + own_f[1] * other_f[1]  18.1 us
    unnamed x15, local copies, waits for them, and re-layouts  17.4 us
    sub x3, other arithmetic, complex_product(): left_re * right_re - left_im * right_im  10.4 us
    all_to_all x1, starting transfers between devices, per_device(): lax.all_to_all(compressed, 'pulse', split_axis=1, concat_axis=2, tiled=True)  7.65 us
  transfers between devices with their start and end apart: 3, of which 2 were waited for; matrix products, arithmetic and copies ran while one was open for 2% of the time, Pallas kernels for 0%

commit v1 on v0

--- a/solution.py
+++ b/solution.py
@@ -1,8 +1,12 @@
+import functools
 import math
 
 import jax
 import jax.numpy as jnp
+import numpy as np
 from jax import lax
+from jax.experimental import pallas as pl
+from jax.experimental.pallas import tpu as pltpu
 from jax.sharding import PartitionSpec as P
 
 RNG = 512
@@ -150,9 +154,289 @@
     return (interfere_real, interfere_imag)
 
 
+OUTER = 16
+
+
+def butterflies(values, sign):
+    count = len(values)
+    if count == 1:
+        return values
+    even = butterflies(values[0::2], sign)
+    odd = butterflies(values[1::2], sign)
+    low, high = [], []
+    for k in range(count // 2):
+        e_re, e_im = even[k]
+        o_re, o_im = odd[k]
+        if k == 0:
+            t_re, t_im = o_re, o_im
+        elif 4 * k == count:
+            t_re, t_im = (-o_im, o_re) if sign > 0 else (o_im, -o_re)
+        else:
+            c = math.cos(2.0 * math.pi * k / count)
+            s = sign * math.sin(2.0 * math.pi * k / count)
+            t_re, t_im = o_re * c - o_im * s, o_re * s + o_im * c
+        low.append((e_re + t_re, e_im + t_im))
+        high.append((e_re - t_re, e_im - t_im))
+    return low + high
+
+
+def compress_kernel(block_cols, counts_ref, phase_ref, echo_ref, out_ref, band):
+    step = pl.program_id(0)
+    pulses = echo_ref.shape[1]
+    width = band.shape[2]
+    window = block_cols + TAPS - 1
+
+    @pl.when(step == 0)
+    def _():
+        amplitude = 2.0 / math.sqrt(TAPS)
+        phase = phase_ref[...]
+        for part, table in enumerate((jnp.cos(phase), jnp.sin(phase))):
+            row = jnp.concatenate(
+                [amplitude * table, jnp.zeros((1, width - TAPS), jnp.float32)], axis=1
+            )
+            rows = jnp.broadcast_to(row, (block_cols, width))
+            band[part] = pltpu.roll(rows, 0, 1, stride=1, stride_axis=0).astype(jnp.bfloat16)
+
+    first = counts_ref[1] + step * pulses
+    ids = first + lax.broadcasted_iota(jnp.int32, (1, pulses), 1)
+    keep = ids < counts_ref[0]
+    band_re = band[0, :, :window]
+    band_im = band[1, :, :window]
+    dims = (((1,), (1,)), ((), ()))
+    dot = functools.partial(
+        lax.dot_general, dimension_numbers=dims, preferred_element_type=jnp.float32
+    )
+    per = out_ref.shape[2]
+    slabs = block_cols // per
+    for block in range(RNG // block_cols):
+        lanes = pl.ds(block * block_cols, window)
+        e_re = echo_ref[0, :, lanes]
+        e_im = echo_ref[1, :, lanes]
+        y_re = dot(band_re, e_re) + dot(band_im, e_im)
+        y_im = dot(band_re, e_im) - dot(band_im, e_re)
+        for part, y in enumerate((y_re, y_im)):
+            kept = jnp.where(keep, y, 0.0).astype(jnp.bfloat16)
+            out_ref[pl.ds(block * slabs, slabs), part] = kept.reshape(slabs, per, pulses)
+
+
+def compress_call(echoes, phase, counts, devices):
+    pulses = echoes.shape[1]
+    step = min(256, pulses)
+    block_cols = 256
+    width = -(-(block_cols + TAPS - 1) // 128) * 128
+    per = RNG // devices
+    return pl.pallas_call(
+        functools.partial(compress_kernel, block_cols),
+        grid=(pulses // step,),
+        out_shape=jax.ShapeDtypeStruct((devices, 2, per, pulses), jnp.bfloat16),
+        in_specs=[
+            pl.BlockSpec(memory_space=pltpu.SMEM),
+            pl.BlockSpec((1, TAPS), lambda i: (0, 0)),
+            pl.BlockSpec((2, step, echoes.shape[2]), lambda i: (0, i, 0)),
+        ],
+        out_specs=pl.BlockSpec((devices, 2, per, step), lambda i: (0, 0, 0, i)),
+        scratch_shapes=[pltpu.VMEM((2, block_cols, width), jnp.bfloat16)],
+        compiler_params=pltpu.CompilerParams(vmem_limit_bytes=48 * 2**20),
+        name="compress",
+    )(counts, phase, echoes)
+
+
+def focus_kernel(
+    acqs, pairs, x_ref, filt_ref, twist_ref, fwd_ref, inv_ref, pool_ref, look_ref, out_ref,
+    held, image, prods,
+):
+    rows = x_ref.shape[2]
+    local = x_ref.shape[3]
+    inner = twist_ref.shape[2]
+    per_src = local // inner
+    chunk = 128
+
+    def forward(index, carry):
+        acq, at = index // (inner // chunk), index % (inner // chunk)
+        values = []
+        for a in range(OUTER):
+            src = (a // per_src) * acqs + acq
+            lane = pl.multiple_of((a % per_src) * inner + at * chunk, chunk)
+            values.append(
+                tuple(
+                    x_ref[src, part, :, pl.ds(lane, chunk)].astype(jnp.float32)
+                    for part in range(2)
+                )
+            )
+        lane = pl.multiple_of(at * chunk, chunk)
+        for k, (re, im) in enumerate(butterflies(values, -1)):
+            c = twist_ref[0, pl.ds(k, 1), pl.ds(lane, chunk)]
+            s = twist_ref[1, pl.ds(k, 1), pl.ds(lane, chunk)]
+            held[acq, k, :, pl.ds(lane, chunk)] = (re * c + im * s).astype(jnp.bfloat16)
+            lane_im = pl.multiple_of(lane + inner, chunk)
+            held[acq, k, :, pl.ds(lane_im, chunk)] = (im * c - re * s).astype(jnp.bfloat16)
+        return carry
+
+    def middle(acq, carry):
+        spec = jnp.dot(
+            held[acq].reshape(OUTER * rows, 2 * inner),
+            fwd_ref[...],
+            preferred_element_type=jnp.float32,
+        )
+        s_re, s_im = spec[:, :inner], spec[:, inner:]
+        f_re = filt_ref[0].reshape(OUTER * rows, inner)
+        f_im = filt_ref[1].reshape(OUTER * rows, inner)
+        m_re = (s_re * f_re - s_im * f_im).astype(jnp.bfloat16)
+        m_im = (s_re * f_im + s_im * f_re).astype(jnp.bfloat16)
+        back = jnp.dot(
+            jnp.concatenate([m_re, m_im], axis=1), inv_ref[...],
+            preferred_element_type=jnp.float32,
+        )
+        image[acq] = back.reshape(OUTER, rows, 2 * inner)
+        return carry
+
+    def inverse(index, carry):
+        acq, at = index // (inner // chunk), index % (inner // chunk)
+        lane = pl.multiple_of(at * chunk, chunk)
+        lane_im = pl.multiple_of(lane + inner, chunk)
+        values = []
+        for k in range(OUTER):
+            re = image[acq, k, :, pl.ds(lane, chunk)]
+            im = image[acq, k, :, pl.ds(lane_im, chunk)]
+            c = twist_ref[0, pl.ds(k, 1), pl.ds(lane, chunk)]
+            s = twist_ref[1, pl.ds(k, 1), pl.ds(lane, chunk)]
+            values.append((re * c - im * s, im * c + re * s))
+        for a, (re, im) in enumerate(butterflies(values, 1)):
+            image[acq, a, :, pl.ds(lane, chunk)] = re
+            image[acq, a, :, pl.ds(lane_im, chunk)] = im
+        return carry
+
+    lax.fori_loop(0, acqs * (inner // chunk), forward, 0)
+    lax.fori_loop(0, acqs, middle, 0)
+    lax.fori_loop(0, acqs * (inner // chunk), inverse, 0)
+
+    group = pool_ref.shape[0] // inner
+    count = len(pairs) * rows
+    parts = [[], []]
+    for g in range(OUTER // group):
+        for step in range(group):
+            a = g * group + step
+            lanes = pl.ds(step * inner, inner)
+            for n, (one, two) in enumerate(pairs):
+                o_re, o_im = image[one, a, :, :inner], image[one, a, :, inner:]
+                t_re, t_im = image[two, a, :, :inner], image[two, a, :, inner:]
+                for part, p in enumerate(
+                    (o_re * t_re + o_im * t_im, o_im * t_re - o_re * t_im)
+                ):
+                    top = p.astype(jnp.bfloat16)
+                    rest = (p - top.astype(jnp.float32)).astype(jnp.bfloat16)
+                    at = part * count + n * rows
+                    prods[pl.ds(at, rows), lanes] = top
+                    prods[pl.ds(2 * count + at, rows), lanes] = rest
+        z = jnp.dot(prods[...], pool_ref[...], preferred_element_type=jnp.float32)
+        z = z[: 2 * count] + z[2 * count :]
+        parts[0].append(z[:count])
+        parts[1].append(z[count:])
+    for part in range(2):
+        out_ref[part] = jnp.dot(
+            look_ref[part], jnp.concatenate(parts[part], axis=1),
+            preferred_element_type=jnp.float32, precision=lax.Precision.HIGHEST,
+        )
+
+
+def focus_tables(acqs, rows, length):
+    inner = length // OUTER
+    b = np.arange(inner)
+    angle = 2.0 * np.pi * (b[:, None] * b[None, :] % inner) / inner
+    c, s = np.cos(angle), np.sin(angle)
+    fwd = np.block([[c, -s], [s, c]]).astype(jnp.bfloat16)
+    inv = np.block([[c, s], [-s, c]]).astype(jnp.bfloat16)
+    angle = 2.0 * np.pi * (np.arange(OUTER)[:, None] * b[None, :]) / length
+    twist = np.stack([np.cos(angle), np.sin(angle)]).astype(np.float32)
+    span = 128 * LOOK_AZ
+    pool = (np.arange(span)[:, None] // LOOK_AZ == np.arange(128)[None, :]).astype(jnp.bfloat16)
+    bits = acqs.bit_length() - 1
+    pairs = [(a, a ^ 1 << bit) for bit in range(bits) for a in range(acqs) if not a >> bit & 1]
+    looks = rows // LOOK_RNG
+    look = np.zeros((2, acqs, bits, looks, len(pairs), rows), np.float32)
+    scale = 1.0 / (LOOK_RNG * LOOK_AZ)
+    for n, (one, two) in enumerate(pairs):
+        bit = (one ^ two).bit_length() - 1
+        for r in range(rows):
+            l = r // LOOK_RNG
+            look[:, one, bit, l, n, r] = scale
+            look[0, two, bit, l, n, r] = scale
+            look[1, two, bit, l, n, r] = -scale
+    look = look.reshape(2, acqs * bits * looks, len(pairs) * rows)
+    return pairs, twist, fwd, inv, pool, look
+
+
+def matched_filter(rate, length):
+    inner = length // OUTER
+    index = (
+        jnp.arange(OUTER, dtype=jnp.int32)[:, None]
+        + OUTER * jnp.arange(inner, dtype=jnp.int32)[None, :]
+    )
+    signed = jnp.where(index < length // 2, index, index - length).astype(jnp.float32)
+    quad = signed * signed / length
+    phase = (jnp.pi * rate)[None, :, None] * quad[:, None, :]
+    return jnp.stack([jnp.cos(phase), -jnp.sin(phase)]) / length
+
+
+def focus_call(x, filt, acqs):
+    rows, local = x.shape[2], x.shape[3]
+    length = x.shape[0] // acqs * local
+    inner = length // OUTER
+    pairs, twist, fwd, inv, pool, look = focus_tables(acqs, rows, length)
+    return pl.pallas_call(
+        functools.partial(focus_kernel, acqs, pairs),
+        out_shape=jax.ShapeDtypeStruct((2, look.shape[1], length // LOOK_AZ), jnp.float32),
+        in_specs=[pl.BlockSpec(memory_space=pltpu.VMEM)] * 7,
+        out_specs=pl.BlockSpec(memory_space=pltpu.VMEM),
+        scratch_shapes=[
+            pltpu.VMEM((acqs, OUTER, rows, 2 * inner), jnp.bfloat16),
+            pltpu.VMEM((acqs, OUTER, rows, 2 * inner), jnp.float32),
+            pltpu.VMEM((4 * len(pairs) * rows, pool.shape[0]), jnp.bfloat16),
+        ],
+        compiler_params=pltpu.CompilerParams(vmem_limit_bytes=48 * 2**20),
+        name="focus",
+    )(x, filt, jnp.asarray(twist), jnp.asarray(fwd), jnp.asarray(inv), jnp.asarray(pool),
+      jnp.asarray(look))
+
+
+def per_device_joint(raw_echo, chirp_phase, pulse_counts, azimuth_rate, partner_bits):
+    echoes = raw_echo[0]
+    pulses_dev = echoes.shape[1]
+    acqs, turns = lax.axis_size("acq"), lax.axis_size("pulse")
+    bits = acqs.bit_length() - 1
+    rows = RNG // (acqs * turns)
+    looks = rows // LOOK_RNG
+    first = lax.axis_index("pulse") * pulses_dev
+    counts = jnp.stack([pulse_counts[0], first.astype(jnp.int32)])
+    y = compress_call(echoes, chirp_phase[None], counts, acqs * turns)
+    x = lax.all_to_all(y, ("pulse", "acq"), split_axis=0, concat_axis=0, tiled=True)
+    rate = lax.dynamic_slice(azimuth_rate, (lax.axis_index("acq") * rows,), (rows,))
+    filt = matched_filter(rate, pulses_dev * turns)
+    out = focus_call(x, filt, acqs)
+    cells = out.shape[2]
+    out = out.reshape(2, acqs, bits * looks, cells)
+    out = lax.all_to_all(out, "acq", split_axis=1, concat_axis=1, tiled=True)
+    out = out.reshape(2, acqs, bits, looks, cells).transpose(0, 2, 1, 3, 4)
+    out = out.reshape(2, bits, acqs * looks, cells)
+    chosen = partner_bits[0]
+    slots = []
+    for slot in range(2):
+        taken = out[:, 0]
+        for which in range(1, bits):
+            taken = jnp.where(chosen[slot] == which, out[:, which], taken)
+        slots.append(taken)
+    return (
+        jnp.stack([item[0] for item in slots])[None],
+        jnp.stack([item[1] for item in slots])[None],
+    )
+
+
 def solution(mesh):
     in_specs = (P("acq", None, "pulse", None), P(), P("acq"), P("pulse"), P("acq", None))
     out_specs = (P("acq", None, "pulse", None), P("acq", None, "pulse", None))
+    devices = mesh.shape["acq"] * mesh.shape["pulse"]
+    joint = RNG % (16 * devices) == 0
     return jax.shard_map(
-        per_device, mesh=mesh, in_specs=in_specs, out_specs=out_specs, check_vma=False
-    )
+        per_device_joint if joint else per_device,
+        mesh=mesh, in_specs=in_specs, out_specs=out_specs, check_vma=False,
+    )

time: 254 us -> 110 us (0.43); the launches traced: 249 us -> 109 us
  local copies, waits for them, and re-layouts: 77.5 us -> 21.6 us
  other arithmetic: 50.7 us -> 3.48 us
  waiting for transfers between devices: 89.8 us -> 49.4 us
  Pallas kernels: 0 us -> 21 us
  matrix products: 19.1 us -> 0 us
    ppermute x2 -> x0, waiting for transfers between devices: 42.8 us -> none  [partner_2(): lax.ppermute(shard, axis, [(i, i ^ 1 << bit) for i in range(lax.axis_size...]
    reduce_sum x4 -> x0, other arithmetic: 28.4 us -> none  [multilook(): return jnp.mean(shaped, axis=(1, 3))]
    pallas_call x0 -> x2, Pallas kernels: none -> 21 us  [the longest x1 12.8 us: focus_call(): pl.pallas_call(functools.partial(focus_kernel, acqs, pairs), out_shape=ja...]
    sub x2 -> x0, local copies, waits for them, and re-layouts: 19.3 us -> none  [cross_looks(): prod_im = own_f[1] * other_f[0] - own_f[0] * other_f[1]]
    dot_general x6 -> x0, matrix products: 19.1 us -> none  [the longest x2 5.93 us: compress(): lax.dot_general(toeplitz, stacked, (((1,), (1,)), ((), ())), preferred_el...]
    add x2 -> x0, local copies, waits for them, and re-layouts: 18.1 us -> none  [cross_looks(): prod_re = own_f[0] * other_f[0] + own_f[1] * other_f[1]]
    sub x4 -> x0, other arithmetic: 14.3 us -> none  [the longest x3 10.4 us: complex_product(): left_re * right_re - left_im * right_im]
    convert_element_type x2 -> x0, local copies, waits for them, and re-layouts: 5.81 us -> none  [the longest x1 3.49 us: compress(): return (joined * keep[None, None, :]).astype(jnp.bfloat16)]
  transfers between devices with their start and end apart: 3 -> 2, of which waited for: 2 -> 2; matrix products, arithmetic and copies ran while one was open for 2% -> 2% of each run, Pallas kernels for 0% -> 0%
where the time goes in v1:
time: 110 us; the launch traced here: 109 us
  waiting for transfers between devices  49.4 us (45%)
  local copies, waits for them, and re-layouts  21.6 us (20%)
  Pallas kernels  21 us (19%)
  starting transfers between devices  10.6 us (10%)
  other arithmetic  3.48 us (3%)
  between operations  2.72 us (2%)
    all_to_all x1, waiting for transfers between devices, per_device_joint(): lax.all_to_all(y, ('pulse', 'acq'), split_axis=0, concat_axis=0, tiled=True)  46.7 us
    unnamed x17, local copies, waits for them, and re-layouts  20.3 us
    pallas_call x1, Pallas kernels, focus_call(): pl.pallas_call(functools.partial(focus_kernel, acqs, pairs), out_shape=ja...  12.8 us
    pallas_call x1, Pallas kernels, compress_call(): pl.pallas_call(functools.partial(compress_kernel, block_cols), grid=(puls...  8.23 us
    all_to_all x1, starting transfers between devices, per_device_joint(): lax.all_to_all(y, ('pulse', 'acq'), split_axis=0, concat_axis=0, tiled=True)  7.29 us
    all_to_all x1, starting transfers between devices, per_device_joint(): out = lax.all_to_all(out, 'acq', split_axis=1, concat_axis=1, tiled=True)  3.32 us
    all_to_all x1, waiting for transfers between devices, per_device_joint(): out = lax.all_to_all(out, 'acq', split_axis=1, concat_axis=1, tiled=True)  2.7 us
  transfers between devices with their start and end apart: 2, of which 2 were waited for; matrix products, arithmetic and copies ran while one was open for 2% of the time, Pallas kernels for 0%

profile of v1, /device:TPU:0, one launch (start us, length us, event | category | flops | bytes accessed | tf_op | source)
XLA Modules:
  0.0 108.9 jit_solution(13203929552096378725)
XLA Ops:
  1.3 0.0 copy-start.5
  1.3 16.3 %copy.14 = bf16[1,2,1024,1535]{3,2,1,0:T(8,128)(2,1)} copy(bf16[1,2,1024,1535]{2,1,3,0:T(2,128)(2,1)} %param.10) | data formatting | bytes 12574720 | tf_op args[0]
  17.6 0.1 pad_add_fusion.counts_ref
  17.6 0.0 copy-done.5
  17.6 8.2 %compress.1 = bf16[32,2,16,1024]{3,2,1,0:T(8,128)(2,1)S(1)} custom-call(s32[2]{0:T(128)S(1)} %pad_add_fusion.counts_ref, f32[1,1024]{1,0:T(1,128)S(1)} %bitcast.24, bf16[2,1024,1535]{2,1,0:T(8,128)(2,1)} %bitcast.25), custom_call_target="tpu_custom_call" | custom-call | tf_op jit(solution)/shard_map/compress/pallas_call | solution.py:228
  25.9 0.0 copy-start
  25.9 1.3 %copy-done = bf16[32,2,16,1024]{3,2,1,0:T(8,128)(2,1)} copy-done((bf16[32,2,16,1024]{3,2,1,0:T(8,128)(2,1)}, bf16[32,2,16,1024]{3,2,1,0:T(8,128)(2,1)S(1)}, u32[]{:S(2)}) %copy-start) | copy-done | bytes 2097176
  27.2 0.0 copy-start.7
  27.2 7.3 %all-to-all-start = ((bf16[32,2,16,1024]{3,2,1,0:T(8,128)(2,1)}), bf16[32,2,16,1024]{3,2,1,0:T(8,128)(2,1)S(1)}, u32[]{:S(2)}, u32[]{:S(2)}) async-start(bf16[32,2,16,1024]{3,2,1,0:T(8,128)(2,1)} %copy-done), calls=%async_computation | async-start | bytes 4194304 | tf_op jit(solution)/shard_map/all_to_all | solution.py:412
  34.5 0.0 copy-start.3
  34.5 0.0 copy-start.4
  34.6 0.0 copy-done.7
  34.6 0.1 dynamic-slice_multiply_fusion
  34.7 1.9 %multiply_cosine_fusion = (f32[1,16,16,512]{3,2,1,0:T(8,128)S(1)}, f32[1,16,16,512]{3,2,1,0:T(8,128)S(1)}) fusion(f32[16,512]{1,0:T(8,128)S(1)} %fusion.3, f32[16]{0:T(128)S(1)} %dynamic-slice_multiply_fusion), kind=kLoop, calls=%fused_computation.2 | loop fusion | flops 262144 | bytes 1081408 | tf_op jit(solution)/shard_map/cos | solution.py:378
  36.6 0.1 maximum_multiply_fusion.filt_ref
  36.7 46.7 %all-to-all-done.x_ref = bf16[32,2,16,1024]{3,2,1,0:T(8,128)(2,1)S(1)} async-done(((bf16[32,2,16,1024]{3,2,1,0:T(8,128)(2,1)}), bf16[32,2,16,1024]{3,2,1,0:T(8,128)(2,1)S(1)}, u32[]{:S(2)}, u32[]{:S(2)}) %all-to-all-start) | async-done | bytes 2097184 | tf_op jit(solution)/shard_map/all_to_all | solution.py:412
  83.4 0.0 copy-done.3
  83.4 0.0 copy-done.4
  83.4 0.0 copy-start.1
  83.4 1.6 %copy-done.1 = bf16[1024,1024]{1,0:T(8,128)(2,1)S(1)} copy-done((bf16[1024,1024]{1,0:T(8,128)(2,1)S(1)}, bf16[1024,1024]{1,0:T(8,128)(2,1)}, u32[]{:S(2)}) %copy-start.1) | copy-done | bytes 2097176
  85.0 0.0 copy-start.2
  85.0 1.0 copy-done.2
  86.1 0.0 copy-start.6
  86.1 12.8 %focus.1 = f32[2,32,512]{2,1,0:T(8,128)S(1)} custom-call(bf16[32,2,16,1024]{3,2,1,0:T(8,128)(2,1)S(1)} %all-to-all-done.x_ref, f32[2,16,16,512]{3,2,1,0:T(8,128)S(1)} %maximum_multiply_fusion.filt_ref, f32[2,16,512]{2,1,0:T(8,128)S(1)} %copy-done.3, bf16[1024,1024]{1,0:T(8,128)(2,1)S(1)} %copy-done.1, bf16[1024,1024]{1,0:T(8,128)(2,1)} %constant.45.clone.inv_ref, ...), custom_call_target="tpu_custom_call" | custom-call | tf_op jit(solution)/shard_map/focus/pallas_call | solution.py:386
  98.8 0.7 copy.15
  99.5 3.3 %all-to-all-start.1 = ((f32[2,4,8,512]{3,2,0,1:T(8,128)}), f32[2,4,8,512]{3,2,0,1:T(8,128)S(1)}, u32[]{:S(2)}, u32[]{:S(2)}) async-start(f32[2,4,8,512]{3,2,0,1:T(8,128)} %copy.15), calls=%async_computation.1 | async-start | bytes 262144 | tf_op jit(solution)/shard_map/all_to_all | solution.py:418
  102.8 0.0 copy-done.6
  102.9 0.6 fusion.4
  104.7 2.7 %all-to-all-done.1 = f32[2,4,8,512]{3,2,0,1:T(8,128)S(1)} async-done(((f32[2,4,8,512]{3,2,0,1:T(8,128)}), f32[2,4,8,512]{3,2,0,1:T(8,128)S(1)}, u32[]{:S(2)}, u32[]{:S(2)}) %all-to-all-start.1) | async-done | bytes 131104 | tf_op jit(solution)/shard_map/all_to_all | solution.py:418
  107.6 0.6 maximum_bitcast_fusion
  108.2 0.6 maximum_bitcast_fusion.1
  (7 shorter events, 0.1 us)
Async XLA Ops:
  1.3 16.4 %copy-start.5 = (f32[1024]{0:T(1024)S(1)}, f32[1024]{0:T(1024)}, u32[]{:S(2)}) copy-start(f32[1024]{0:T(1024)} %param.11) | copy-start | bytes 12292
  25.9 1.3 %copy-start = (bf16[32,2,16,1024]{3,2,1,0:T(8,128)(2,1)}, bf16[32,2,16,1024]{3,2,1,0:T(8,128)(2,1)S(1)}, u32[]{:S(2)}) copy-start(bf16[32,2,16,1024]{3,2,1,0:T(8,128)(2,1)S(1)} %compress.1) | copy-start | bytes 6291460
  27.2 7.3 %copy-start.7 = (f32[64]{0:T(128)S(1)}, f32[64]{0:T(128)}, u32[]{:S(2)}) copy-start(f32[64]{0:T(128)} %param.13) | copy-start | bytes 772
  27.2 56.2 %all-to-all-start = ((bf16[32,2,16,1024]{3,2,1,0:T(8,128)(2,1)}), bf16[32,2,16,1024]{3,2,1,0:T(8,128)(2,1)S(1)}, u32[]{:S(2)}, u32[]{:S(2)}) async-start(bf16[32,2,16,1024]{3,2,1,0:T(8,128)(2,1)} %copy-done), calls=%async_computation | async-start | bytes 4194304 | tf_op jit(solution)/shard_map/all_to_all | solution.py:412
  34.5 48.9 %copy-start.3 = (f32[2,16,512]{2,1,0:T(8,128)S(1)}, f32[2,16,512]{2,1,0:T(8,128)}, u32[]{:S(2)}) copy-start(f32[2,16,512]{2,1,0:T(8,128)} %constant.43.clone.twist_ref) | copy-start | bytes 196612
  34.5 48.9 %copy-start.4 = (f32[2,32,64]{2,1,0:T(8,128)S(1)}, f32[2,32,64]{2,1,0:T(8,128)}, u32[]{:S(2)}) copy-start(f32[2,32,64]{2,1,0:T(8,128)} %constant.47.clone.look_ref) | copy-start | bytes 49156
  83.4 1.6 %copy-start.1 = (bf16[1024,1024]{1,0:T(8,128)(2,1)S(1)}, bf16[1024,1024]{1,0:T(8,128)(2,1)}, u32[]{:S(2)}) copy-start(bf16[1024,1024]{1,0:T(8,128)(2,1)} %constant.44.clone.fwd_ref) | copy-start | bytes 6291460
  85.0 1.0 copy-start.2
  86.1 16.8 %copy-start.6 = (s32[1,2]{1,0:T(1,128)S(1)}, s32[1,2]{1,0:T(1,128)}, u32[]{:S(2)}) copy-start(s32[1,2]{1,0:T(1,128)} %param.14) | copy-start | bytes 28
  99.5 7.9 %all-to-all-start.1 = ((f32[2,4,8,512]{3,2,0,1:T(8,128)}), f32[2,4,8,512]{3,2,0,1:T(8,128)S(1)}, u32[]{:S(2)}, u32[]{:S(2)}) async-start(f32[2,4,8,512]{3,2,0,1:T(8,128)} %copy.15), calls=%async_computation.1 | async-start | bytes 262144 | tf_op jit(solution)/shard_map/all_to_all | solution.py:418

commit v2 on v1

--- a/solution.py
+++ b/solution.py
@@ -182,7 +182,7 @@
 
 def compress_kernel(block_cols, counts_ref, phase_ref, echo_ref, out_ref, band):
     step = pl.program_id(0)
-    pulses = echo_ref.shape[1]
+    pulses = echo_ref.shape[2]
     width = band.shape[2]
     window = block_cols + TAPS - 1
 
@@ -190,40 +190,37 @@
     def _():
         amplitude = 2.0 / math.sqrt(TAPS)
         phase = phase_ref[...]
-        for part, table in enumerate((jnp.cos(phase), jnp.sin(phase))):
+        cosine, sine = amplitude * jnp.cos(phase), amplitude * jnp.sin(phase)
+        even = lax.broadcasted_iota(jnp.int32, phase.shape, 1) % 2 == 0
+        for part, table in enumerate(
+            (jnp.where(even, cosine, sine), jnp.where(even, -sine, cosine))
+        ):
             row = jnp.concatenate(
-                [amplitude * table, jnp.zeros((1, width - TAPS), jnp.float32)], axis=1
+                [table, jnp.zeros((1, width - 2 * TAPS), jnp.float32)], axis=1
             )
             rows = jnp.broadcast_to(row, (block_cols, width))
-            band[part] = pltpu.roll(rows, 0, 1, stride=1, stride_axis=0).astype(jnp.bfloat16)
+            band[part] = pltpu.roll(rows, 0, 1, stride=2, stride_axis=0).astype(jnp.bfloat16)
 
     first = counts_ref[1] + step * pulses
     ids = first + lax.broadcasted_iota(jnp.int32, (1, pulses), 1)
     keep = ids < counts_ref[0]
-    band_re = band[0, :, :window]
-    band_im = band[1, :, :window]
-    dims = (((1,), (1,)), ((), ()))
-    dot = functools.partial(
-        lax.dot_general, dimension_numbers=dims, preferred_element_type=jnp.float32
-    )
     per = out_ref.shape[2]
     slabs = block_cols // per
     for block in range(RNG // block_cols):
-        lanes = pl.ds(block * block_cols, window)
-        e_re = echo_ref[0, :, lanes]
-        e_im = echo_ref[1, :, lanes]
-        y_re = dot(band_re, e_re) + dot(band_im, e_im)
-        y_im = dot(band_re, e_im) - dot(band_im, e_re)
-        for part, y in enumerate((y_re, y_im)):
+        echo = echo_ref[pl.ds(block * block_cols, window)].reshape(2 * window, pulses)
+        for part in range(2):
+            y = jnp.dot(
+                band[part, :, : 2 * window], echo, preferred_element_type=jnp.float32
+            )
             kept = jnp.where(keep, y, 0.0).astype(jnp.bfloat16)
             out_ref[pl.ds(block * slabs, slabs), part] = kept.reshape(slabs, per, pulses)
 
 
 def compress_call(echoes, phase, counts, devices):
-    pulses = echoes.shape[1]
+    pulses = echoes.shape[2]
     step = min(256, pulses)
     block_cols = 256
-    width = -(-(block_cols + TAPS - 1) // 128) * 128
+    width = -(-2 * (block_cols + TAPS - 1) // 128) * 128
     per = RNG // devices
     return pl.pallas_call(
         functools.partial(compress_kernel, block_cols),
@@ -231,8 +228,8 @@
         out_shape=jax.ShapeDtypeStruct((devices, 2, per, pulses), jnp.bfloat16),
         in_specs=[
             pl.BlockSpec(memory_space=pltpu.SMEM),
-            pl.BlockSpec((1, TAPS), lambda i: (0, 0)),
-            pl.BlockSpec((2, step, echoes.shape[2]), lambda i: (0, i, 0)),
+            pl.BlockSpec((1, 2 * TAPS), lambda i: (0, 0)),
+            pl.BlockSpec((echoes.shape[0], 2, step), lambda i: (0, 0, i)),
         ],
         out_specs=pl.BlockSpec((devices, 2, per, step), lambda i: (0, 0, 0, i)),
         scratch_shapes=[pltpu.VMEM((2, block_cols, width), jnp.bfloat16)],
@@ -400,15 +397,15 @@
 
 
 def per_device_joint(raw_echo, chirp_phase, pulse_counts, azimuth_rate, partner_bits):
-    echoes = raw_echo[0]
-    pulses_dev = echoes.shape[1]
+    echoes = raw_echo[0].transpose(2, 0, 1)
+    pulses_dev = echoes.shape[2]
     acqs, turns = lax.axis_size("acq"), lax.axis_size("pulse")
     bits = acqs.bit_length() - 1
     rows = RNG // (acqs * turns)
     looks = rows // LOOK_RNG
     first = lax.axis_index("pulse") * pulses_dev
     counts = jnp.stack([pulse_counts[0], first.astype(jnp.int32)])
-    y = compress_call(echoes, chirp_phase[None], counts, acqs * turns)
+    y = compress_call(echoes, jnp.repeat(chirp_phase, 2)[None], counts, acqs * turns)
     x = lax.all_to_all(y, ("pulse", "acq"), split_axis=0, concat_axis=0, tiled=True)
     rate = lax.dynamic_slice(azimuth_rate, (lax.axis_index("acq") * rows,), (rows,))
     filt = matched_filter(rate, pulses_dev * turns)

time: 110 us -> 94.3 us (0.86)
  local copies, waits for them, and re-layouts: 21.6 us -> 6.54 us
    unnamed x17 -> x14, local copies, waits for them, and re-layouts: 20.3 us -> 3.99 us
  transfers between devices with their start and end apart: 2 -> 2, of which waited for: 2 -> 2; matrix products, arithmetic and copies ran while one was open for 2% -> 3% of each run, Pallas kernels for 0% -> 0%
where the time goes in v2:
time: 94.3 us; the launch traced here: 93.8 us
  waiting for transfers between devices  49.4 us (52%)
  Pallas kernels  21 us (22%)
  starting transfers between devices  10.6 us (11%)
  local copies, waits for them, and re-layouts  6.54 us (7%)
  other arithmetic  3.48 us (4%)
  between operations  2.72 us (3%)
    all_to_all x1, waiting for transfers between devices, per_device_joint(): lax.all_to_all(y, ('pulse', 'acq'), split_axis=0, concat_axis=0, tiled=True)  46.7 us
    pallas_call x1, Pallas kernels, focus_call(): pl.pallas_call(functools.partial(focus_kernel, acqs, pairs), out_shape=ja...  12.8 us
    pallas_call x1, Pallas kernels, compress_call(): pl.pallas_call(functools.partial(compress_kernel, block_cols), grid=(puls...  8.22 us
    all_to_all x1, starting transfers between devices, per_device_joint(): lax.all_to_all(y, ('pulse', 'acq'), split_axis=0, concat_axis=0, tiled=True)  7.29 us
    unnamed x14, local copies, waits for them, and re-layouts  3.99 us
    all_to_all x1, starting transfers between devices, per_device_joint(): out = lax.all_to_all(out, 'acq', split_axis=1, concat_axis=1, tiled=True)  3.32 us
    all_to_all x1, waiting for transfers between devices, per_device_joint(): out = lax.all_to_all(out, 'acq', split_axis=1, concat_axis=1, tiled=True)  2.7 us
    cos x1, other arithmetic, matched_filter(): return jnp.stack([jnp.cos(phase), -jnp.sin(phase)]) / length  1.9 us
  transfers between devices with their start and end apart: 2, of which 2 were waited for; matrix products, arithmetic and copies ran while one was open for 3% of the time, Pallas kernels for 0%

profile of v2, /device:TPU:0, one launch (start us, length us, event | category | flops | bytes accessed | tf_op | source)
XLA Modules:
  0.0 93.8 jit_solution(3971889141974323583)
XLA Ops:
  1.3 0.9 broadcast_in_dim.6
  2.2 0.3 broadcast_in_dim_reshape.3.phase_ref
  2.5 0.1 pad_add_fusion.counts_ref
  2.6 8.2 %compress.1 = bf16[32,2,16,1024]{3,2,1,0:T(8,128)(2,1)S(1)} custom-call(s32[2]{0:T(128)S(1)} %pad_add_fusion.counts_ref, f32[1,2048]{1,0:T(1,128)S(1)} %broadcast_in_dim_reshape.3.phase_ref, bf16[1535,2,1024]{2,1,0:T(2,128)(2,1)} %bitcast.25), custom_call_target="tpu_custom_call" | custom-call | tf_op jit(solution)/shard_map/compress/pallas_call | solution.py:225
  10.8 0.0 copy-start
  10.8 1.3 %copy-done = bf16[32,2,16,1024]{3,2,1,0:T(8,128)(2,1)} copy-done((bf16[32,2,16,1024]{3,2,1,0:T(8,128)(2,1)}, bf16[32,2,16,1024]{3,2,1,0:T(8,128)(2,1)S(1)}, u32[]{:S(2)}) %copy-start) | copy-done | bytes 2097176
  12.1 0.0 copy-start.6
  12.1 7.3 %all-to-all-start = ((bf16[32,2,16,1024]{3,2,1,0:T(8,128)(2,1)}), bf16[32,2,16,1024]{3,2,1,0:T(8,128)(2,1)S(1)}, u32[]{:S(2)}, u32[]{:S(2)}) async-start(bf16[32,2,16,1024]{3,2,1,0:T(8,128)(2,1)} %copy-done), calls=%async_computation | async-start | bytes 4194304 | tf_op jit(solution)/shard_map/all_to_all | solution.py:409
  19.4 0.0 copy-start.3
  19.4 0.0 copy-start.4
  19.5 0.0 copy-done.6
  19.5 0.1 dynamic-slice_multiply_fusion
  19.6 1.9 %multiply_cosine_fusion = (f32[1,16,16,512]{3,2,1,0:T(8,128)S(1)}, f32[1,16,16,512]{3,2,1,0:T(8,128)S(1)}) fusion(f32[16,512]{1,0:T(8,128)S(1)} %fusion.3, f32[16]{0:T(128)S(1)} %dynamic-slice_multiply_fusion), kind=kLoop, calls=%fused_computation.2 | loop fusion | flops 262144 | bytes 1081408 | tf_op jit(solution)/shard_map/cos | solution.py:375
  21.5 0.1 maximum_multiply_fusion.filt_ref
  21.6 46.7 %all-to-all-done.x_ref = bf16[32,2,16,1024]{3,2,1,0:T(8,128)(2,1)S(1)} async-done(((bf16[32,2,16,1024]{3,2,1,0:T(8,128)(2,1)}), bf16[32,2,16,1024]{3,2,1,0:T(8,128)(2,1)S(1)}, u32[]{:S(2)}, u32[]{:S(2)}) %all-to-all-start) | async-done | bytes 2097184 | tf_op jit(solution)/shard_map/all_to_all | solution.py:409
  68.3 0.0 copy-done.3
  68.3 0.0 copy-done.4
  68.3 0.0 copy-start.1
  68.3 1.6 %copy-done.1 = bf16[1024,1024]{1,0:T(8,128)(2,1)S(1)} copy-done((bf16[1024,1024]{1,0:T(8,128)(2,1)S(1)}, bf16[1024,1024]{1,0:T(8,128)(2,1)}, u32[]{:S(2)}) %copy-start.1) | copy-done | bytes 2097176
  69.9 0.0 copy-start.2
  69.9 1.0 %copy-done.2 = bf16[2048,128]{1,0:T(8,128)(2,1)S(1)} copy-done((bf16[2048,128]{1,0:T(8,128)(2,1)S(1)}, bf16[2048,128]{1,0:T(8,128)(2,1)}, u32[]{:S(2)}) %copy-start.2) | copy-done | bytes 524312
  71.0 0.0 copy-start.5
  71.0 12.8 %focus.1 = f32[2,32,512]{2,1,0:T(8,128)S(1)} custom-call(bf16[32,2,16,1024]{3,2,1,0:T(8,128)(2,1)S(1)} %all-to-all-done.x_ref, f32[2,16,16,512]{3,2,1,0:T(8,128)S(1)} %maximum_multiply_fusion.filt_ref, f32[2,16,512]{2,1,0:T(8,128)S(1)} %copy-done.3, bf16[1024,1024]{1,0:T(8,128)(2,1)S(1)} %copy-done.1, bf16[1024,1024]{1,0:T(8,128)(2,1)} %constant.45.clone.inv_ref, ...), custom_call_target="tpu_custom_call" | custom-call | tf_op jit(solution)/shard_map/focus/pallas_call | solution.py:383
  83.8 0.7 copy.14
  84.4 3.3 %all-to-all-start.1 = ((f32[2,4,8,512]{3,2,0,1:T(8,128)}), f32[2,4,8,512]{3,2,0,1:T(8,128)S(1)}, u32[]{:S(2)}, u32[]{:S(2)}) async-start(f32[2,4,8,512]{3,2,0,1:T(8,128)} %copy.14), calls=%async_computation.1 | async-start | bytes 262144 | tf_op jit(solution)/shard_map/all_to_all | solution.py:415
  87.8 0.0 copy-done.5
  87.8 0.6 fusion.4
  89.6 2.7 %all-to-all-done.1 = f32[2,4,8,512]{3,2,0,1:T(8,128)S(1)} async-done(((f32[2,4,8,512]{3,2,0,1:T(8,128)}), f32[2,4,8,512]{3,2,0,1:T(8,128)S(1)}, u32[]{:S(2)}, u32[]{:S(2)}) %all-to-all-start.1) | async-done | bytes 131104 | tf_op jit(solution)/shard_map/all_to_all | solution.py:415
  92.5 0.6 maximum_bitcast_fusion
  93.1 0.6 maximum_bitcast_fusion.1
  (7 shorter events, 0.1 us)
Async XLA Ops:
  10.8 1.3 %copy-start = (bf16[32,2,16,1024]{3,2,1,0:T(8,128)(2,1)}, bf16[32,2,16,1024]{3,2,1,0:T(8,128)(2,1)S(1)}, u32[]{:S(2)}) copy-start(bf16[32,2,16,1024]{3,2,1,0:T(8,128)(2,1)S(1)} %compress.1) | copy-start | bytes 6291460
  12.1 7.3 %copy-start.6 = (f32[64]{0:T(128)S(1)}, f32[64]{0:T(128)}, u32[]{:S(2)}) copy-start(f32[64]{0:T(128)} %param.13) | copy-start | bytes 772
  12.1 56.2 %all-to-all-start = ((bf16[32,2,16,1024]{3,2,1,0:T(8,128)(2,1)}), bf16[32,2,16,1024]{3,2,1,0:T(8,128)(2,1)S(1)}, u32[]{:S(2)}, u32[]{:S(2)}) async-start(bf16[32,2,16,1024]{3,2,1,0:T(8,128)(2,1)} %copy-done), calls=%async_computation | async-start | bytes 4194304 | tf_op jit(solution)/shard_map/all_to_all | solution.py:409
  19.4 48.9 %copy-start.3 = (f32[2,16,512]{2,1,0:T(8,128)S(1)}, f32[2,16,512]{2,1,0:T(8,128)}, u32[]{:S(2)}) copy-start(f32[2,16,512]{2,1,0:T(8,128)} %constant.43.clone.twist_ref) | copy-start | bytes 196612
  19.4 48.9 %copy-start.4 = (f32[2,32,64]{2,1,0:T(8,128)S(1)}, f32[2,32,64]{2,1,0:T(8,128)}, u32[]{:S(2)}) copy-start(f32[2,32,64]{2,1,0:T(8,128)} %constant.47.clone.look_ref) | copy-start | bytes 49156
  68.3 1.6 %copy-start.1 = (bf16[1024,1024]{1,0:T(8,128)(2,1)S(1)}, bf16[1024,1024]{1,0:T(8,128)(2,1)}, u32[]{:S(2)}) copy-start(bf16[1024,1024]{1,0:T(8,128)(2,1)} %constant.44.clone.fwd_ref) | copy-start | bytes 6291460
  69.9 1.0 %copy-start.2 = (bf16[2048,128]{1,0:T(8,128)(2,1)S(1)}, bf16[2048,128]{1,0:T(8,128)(2,1)}, u32[]{:S(2)}) copy-start(bf16[2048,128]{1,0:T(8,128)(2,1)} %constant.46.clone.pool_ref) | copy-start | bytes 1572868
  71.0 16.8 %copy-start.5 = (s32[1,2]{1,0:T(1,128)S(1)}, s32[1,2]{1,0:T(1,128)}, u32[]{:S(2)}) copy-start(s32[1,2]{1,0:T(1,128)} %param.14) | copy-start | bytes 28
  84.4 7.9 %all-to-all-start.1 = ((f32[2,4,8,512]{3,2,0,1:T(8,128)}), f32[2,4,8,512]{3,2,0,1:T(8,128)S(1)}, u32[]{:S(2)}, u32[]{:S(2)}) async-start(f32[2,4,8,512]{3,2,0,1:T(8,128)} %copy.14), calls=%async_computation.1 | async-start | bytes 262144 | tf_op jit(solution)/shard_map/all_to_all | solution.py:415

commit v3 on v2

--- a/solution.py
+++ b/solution.py
@@ -180,8 +180,31 @@
     return low + high
 
 
-def compress_kernel(block_cols, counts_ref, phase_ref, echo_ref, out_ref, band):
+def compress_kernel(
+    block_cols, counts_ref, phase_ref, echo_ref, turned_ref, band, ready, send_sem, recv_sem,
+    own_sem,
+):
     step = pl.program_id(0)
+    steps = pl.num_programs(0)
+    acqs = lax.axis_size("acq")
+    devices = acqs * lax.axis_size("pulse")
+    me = lax.axis_index("pulse") * acqs + lax.axis_index("acq")
+    barrier = pltpu.get_barrier_semaphore()
+
+    def place(d):
+        peer = me ^ d
+        return peer, (peer % acqs, peer // acqs)
+
+    @pl.when(step == 0)
+    def _():
+        def greet(d, carry):
+            pl.semaphore_signal(
+                barrier, inc=1, device_id=place(d)[1], device_id_type=pl.DeviceIdType.MESH
+            )
+            return carry
+
+        lax.fori_loop(1, devices, greet, 0)
+
     pulses = echo_ref.shape[2]
     width = band.shape[2]
     window = block_cols + TAPS - 1
@@ -204,7 +227,7 @@
     first = counts_ref[1] + step * pulses
     ids = first + lax.broadcasted_iota(jnp.int32, (1, pulses), 1)
     keep = ids < counts_ref[0]
-    per = out_ref.shape[2]
+    per = ready.shape[3]
     slabs = block_cols // per
     for block in range(RNG // block_cols):
         echo = echo_ref[pl.ds(block * block_cols, window)].reshape(2 * window, pulses)
@@ -213,27 +236,79 @@
                 band[part, :, : 2 * window], echo, preferred_element_type=jnp.float32
             )
             kept = jnp.where(keep, y, 0.0).astype(jnp.bfloat16)
-            out_ref[pl.ds(block * slabs, slabs), part] = kept.reshape(slabs, per, pulses)
+            ready[step, pl.ds(block * slabs, slabs), part] = kept.reshape(slabs, per, pulses)
+
+    @pl.when(step == 0)
+    def _():
+        pl.semaphore_wait(barrier, devices - 1)
+
+    def remote(at, d):
+        peer, where = place(d)
+        lanes = pl.ds(pl.multiple_of(at * pulses, 128), pulses)
+        return pltpu.make_async_remote_copy(
+            src_ref=ready.at[at, peer],
+            dst_ref=turned_ref.at[me, :, :, lanes],
+            send_sem=send_sem.at[at, d],
+            recv_sem=recv_sem.at[at, d],
+            device_id=where,
+            device_id_type=pl.DeviceIdType.MESH,
+        )
+
+    def own(at):
+        lanes = pl.ds(pl.multiple_of(at * pulses, 128), pulses)
+        return pltpu.make_async_copy(
+            ready.at[at, me], turned_ref.at[me, :, :, lanes], own_sem.at[at]
+        )
+
+    half = devices // 2
+
+    def send(i, carry):
+        remote(step, devices - 1 - i).start()
+        remote(step, half - 1 - i).start()
+        return carry
+
+    lax.fori_loop(0, half - 1, send, 0)
+    remote(step, half).start()
+    own(step).start()
+
+    @pl.when(step == steps - 1)
+    def _():
+        def finish(i, carry):
+            remote(i // (devices - 1), i % (devices - 1) + 1).wait()
+            return carry
+
+        lax.fori_loop(0, steps * (devices - 1), finish, 0)
+        for at in range(ready.shape[0]):
+            own(at).wait()
 
 
 def compress_call(echoes, phase, counts, devices):
     pulses = echoes.shape[2]
-    step = min(256, pulses)
+    step = min(512, pulses)
+    steps = pulses // step
     block_cols = 256
     width = -(-2 * (block_cols + TAPS - 1) // 128) * 128
     per = RNG // devices
     return pl.pallas_call(
         functools.partial(compress_kernel, block_cols),
-        grid=(pulses // step,),
+        grid=(steps,),
         out_shape=jax.ShapeDtypeStruct((devices, 2, per, pulses), jnp.bfloat16),
         in_specs=[
             pl.BlockSpec(memory_space=pltpu.SMEM),
             pl.BlockSpec((1, 2 * TAPS), lambda i: (0, 0)),
             pl.BlockSpec((echoes.shape[0], 2, step), lambda i: (0, 0, i)),
         ],
-        out_specs=pl.BlockSpec((devices, 2, per, step), lambda i: (0, 0, 0, i)),
-        scratch_shapes=[pltpu.VMEM((2, block_cols, width), jnp.bfloat16)],
-        compiler_params=pltpu.CompilerParams(vmem_limit_bytes=48 * 2**20),
+        out_specs=pl.BlockSpec(memory_space=pl.ANY),
+        scratch_shapes=[
+            pltpu.VMEM((2, block_cols, width), jnp.bfloat16),
+            pltpu.VMEM((steps, devices, 2, per, step), jnp.bfloat16),
+            pltpu.SemaphoreType.DMA((steps, devices)),
+            pltpu.SemaphoreType.DMA((steps, devices)),
+            pltpu.SemaphoreType.DMA((steps,)),
+        ],
+        compiler_params=pltpu.CompilerParams(
+            vmem_limit_bytes=40 * 2**20, collective_id=0, has_side_effects=True
+        ),
         name="compress",
     )(counts, phase, echoes)
 
@@ -405,8 +480,7 @@
     looks = rows // LOOK_RNG
     first = lax.axis_index("pulse") * pulses_dev
     counts = jnp.stack([pulse_counts[0], first.astype(jnp.int32)])
-    y = compress_call(echoes, jnp.repeat(chirp_phase, 2)[None], counts, acqs * turns)
-    x = lax.all_to_all(y, ("pulse", "acq"), split_axis=0, concat_axis=0, tiled=True)
+    x = compress_call(echoes, jnp.repeat(chirp_phase, 2)[None], counts, acqs * turns)
     rate = lax.dynamic_slice(azimuth_rate, (lax.axis_index("acq") * rows,), (rows,))
     filt = matched_filter(rate, pulses_dev * turns)
     out = focus_call(x, filt, acqs)

time: 94.3 us -> 87.7 us (0.930)
  Pallas kernels: 21 us -> 69.1 us
  waiting for transfers between devices: 49.4 us -> 2.7 us
  starting transfers between devices: 10.6 us -> 3.32 us
  local copies, waits for them, and re-layouts: 6.54 us -> 5.34 us
    pallas_call x1, Pallas kernels: 8.22 us -> 56.3 us  [compress_call(): pl.pallas_call(functools.partial(compress_kernel, block_cols), grid=(step...]
    all_to_all x1 -> x0, waiting for transfers between devices: 46.7 us -> none  [per_device_joint(): lax.all_to_all(y, ('pulse', 'acq'), split_axis=0, concat_axis=0, tiled=True)]
    all_to_all x1 -> x0, starting transfers between devices: 7.29 us -> none  [per_device_joint(): lax.all_to_all(y, ('pulse', 'acq'), split_axis=0, concat_axis=0, tiled=True)]
    unnamed x14 -> x12, local copies, waits for them, and re-layouts: 3.99 us -> 2.8 us
  transfers between devices with their start and end apart: 2 -> 1, of which waited for: 2 -> 1; matrix products, arithmetic and copies ran while one was open for 3% -> 1% of each run, Pallas kernels for 0% -> 0%
where the time goes in v3:
time: 87.7 us; the launch traced here: 87.3 us
  Pallas kernels  69.1 us (79%)
  local copies, waits for them, and re-layouts  5.34 us (6%)
  other arithmetic  4.13 us (5%)
  starting transfers between devices  3.32 us (4%)
  between operations  2.74 us (3%)
  waiting for transfers between devices  2.7 us (3%)
    pallas_call x1, Pallas kernels, compress_call(): pl.pallas_call(functools.partial(compress_kernel, block_cols), grid=(step...  56.3 us
    pallas_call x1, Pallas kernels, focus_call(): pl.pallas_call(functools.partial(focus_kernel, acqs, pairs), out_shape=ja...  12.8 us
    all_to_all x1, starting transfers between devices, per_device_joint(): out = lax.all_to_all(out, 'acq', split_axis=1, concat_axis=1, tiled=True)  3.32 us
    unnamed x12, local copies, waits for them, and re-layouts  2.8 us
    all_to_all x1, waiting for transfers between devices, per_device_joint(): out = lax.all_to_all(out, 'acq', split_axis=1, concat_axis=1, tiled=True)  2.7 us
    cos x1, other arithmetic, matched_filter(): return jnp.stack([jnp.cos(phase), -jnp.sin(phase)]) / length  1.91 us
  transfers between devices with their start and end apart: 1, of which 1 were waited for; matrix products, arithmetic and copies ran while one was open for 1% of the time, Pallas kernels for 0%

profile of v3, /device:TPU:0, one launch (start us, length us, event | category | flops | bytes accessed | tf_op | source)
XLA Modules:
  0.0 87.3 jit_solution(2187053987378611447)
XLA Ops:
  1.3 0.9 %broadcast_in_dim.6 = f32[1024,2]{1,0:T(8,128)S(1)} broadcast(f32[1024]{0:T(1024)} %param.11), dimensions={0} | broadcast | bytes 12288 | tf_op jit(solution)/shard_map/broadcast_in_dim | solution.py:483
  2.2 0.3 broadcast_in_dim_reshape.3.phase_ref
  2.5 0.7 dynamic-slice_multiply_fusion
  3.3 1.9 %multiply_cosine_fusion = (f32[1,16,16,512]{3,2,1,0:T(8,128)S(1)}, f32[1,16,16,512]{3,2,1,0:T(8,128)S(1)}) fusion(f32[16,512]{1,0:T(8,128)S(1)} %fusion.3, f32[16]{0:T(128)S(1)} %dynamic-slice_multiply_fusion), kind=kLoop, calls=%fused_computation.2 | loop fusion | flops 262144 | bytes 1081408 | tf_op jit(solution)/shard_map/cos | solution.py:450
  5.2 0.1 maximum_multiply_fusion.filt_ref
  5.3 0.1 pad_add_fusion.counts_ref
  5.4 0.0 copy-start
  5.4 2.8 %copy-done = bf16[1,2,1024,1535]{2,1,3,0:T(2,128)(2,1)S(1)} copy-done((bf16[1,2,1024,1535]{2,1,3,0:T(2,128)(2,1)S(1)}, bf16[1,2,1024,1535]{2,1,3,0:T(2,128)(2,1)}, u32[]{:S(2)}) %copy-start) | copy-done | bytes 6287384
  8.2 0.0 copy-start.1
  8.2 0.0 copy-start.2
  8.2 0.0 copy-start.3
  8.2 0.0 copy-start.4
  8.2 56.3 %compress.1.x_ref = bf16[32,2,16,1024]{3,2,1,0:T(8,128)(2,1)S(1)} custom-call(s32[2]{0:T(128)S(1)} %pad_add_fusion.counts_ref, f32[1,2048]{1,0:T(1,128)S(1)} %broadcast_in_dim_reshape.3.phase_ref, bf16[1535,2,1024]{2,1,0:T(2,128)(2,1)S(1)} %bitcast.24), custom_call_target="tpu_custom_call" | custom-call | tf_op jit(solution)/shard_map/compress/pallas_call | solution.py:292
  64.5 0.0 copy-done.1
  64.5 0.0 copy-done.2
  64.5 0.0 copy-done.3
  64.5 0.0 copy-done.4
  64.6 0.0 copy-start.5
  64.6 12.8 %focus.1 = f32[2,32,512]{2,1,0:T(8,128)S(1)} custom-call(bf16[32,2,16,1024]{3,2,1,0:T(8,128)(2,1)S(1)} %compress.1.x_ref, f32[2,16,16,512]{3,2,1,0:T(8,128)S(1)} %maximum_multiply_fusion.filt_ref, f32[2,16,512]{2,1,0:T(8,128)S(1)} %copy-done.3, bf16[1024,1024]{1,0:T(8,128)(2,1)S(1)} %copy-done.1, bf16[1024,1024]{1,0:T(8,128)(2,1)} %constant.45.clone.inv_ref, ...), custom_call_target="tpu_custom_call" | custom-call | tf_op jit(solution)/shard_map/focus/pallas_call | solution.py:458
  77.3 0.7 copy.14
  78.0 3.3 %all-to-all-start = ((f32[2,4,8,512]{3,2,0,1:T(8,128)}), f32[2,4,8,512]{3,2,0,1:T(8,128)S(1)}, u32[]{:S(2)}, u32[]{:S(2)}) async-start(f32[2,4,8,512]{3,2,0,1:T(8,128)} %copy.14), calls=%async_computation | async-start | bytes 262144 | tf_op jit(solution)/shard_map/all_to_all | solution.py:489
  81.3 0.0 copy-done.5
  81.3 0.6 fusion.4
  83.2 2.7 %all-to-all-done = f32[2,4,8,512]{3,2,0,1:T(8,128)S(1)} async-done(((f32[2,4,8,512]{3,2,0,1:T(8,128)}), f32[2,4,8,512]{3,2,0,1:T(8,128)S(1)}, u32[]{:S(2)}, u32[]{:S(2)}) %all-to-all-start) | async-done | bytes 131104 | tf_op jit(solution)/shard_map/all_to_all | solution.py:489
  86.1 0.6 maximum_bitcast_fusion.1
  86.7 0.6 maximum_bitcast_fusion
  (7 shorter events, 0.1 us)
Async XLA Ops:
  5.4 2.8 %copy-start = (bf16[1,2,1024,1535]{2,1,3,0:T(2,128)(2,1)S(1)}, bf16[1,2,1024,1535]{2,1,3,0:T(2,128)(2,1)}, u32[]{:S(2)}) copy-start(bf16[1,2,1024,1535]{2,1,3,0:T(2,128)(2,1)} %param.10) | copy-start | bytes 18862084
  8.2 56.4 %copy-start.1 = (bf16[1024,1024]{1,0:T(8,128)(2,1)S(1)}, bf16[1024,1024]{1,0:T(8,128)(2,1)}, u32[]{:S(2)}) copy-start(bf16[1024,1024]{1,0:T(8,128)(2,1)} %constant.44.clone.fwd_ref) | copy-start | bytes 6291460
  8.2 56.4 %copy-start.2 = (bf16[2048,128]{1,0:T(8,128)(2,1)S(1)}, bf16[2048,128]{1,0:T(8,128)(2,1)}, u32[]{:S(2)}) copy-start(bf16[2048,128]{1,0:T(8,128)(2,1)} %constant.46.clone.pool_ref) | copy-start | bytes 1572868
  8.2 56.4 %copy-start.3 = (f32[2,16,512]{2,1,0:T(8,128)S(1)}, f32[2,16,512]{2,1,0:T(8,128)}, u32[]{:S(2)}) copy-start(f32[2,16,512]{2,1,0:T(8,128)} %constant.43.clone.twist_ref) | copy-start | bytes 196612
  8.2 56.4 %copy-start.4 = (f32[2,32,64]{2,1,0:T(8,128)S(1)}, f32[2,32,64]{2,1,0:T(8,128)}, u32[]{:S(2)}) copy-start(f32[2,32,64]{2,1,0:T(8,128)} %constant.47.clone.look_ref) | copy-start | bytes 49156
  64.6 16.8 %copy-start.5 = (s32[1,2]{1,0:T(1,128)S(1)}, s32[1,2]{1,0:T(1,128)}, u32[]{:S(2)}) copy-start(s32[1,2]{1,0:T(1,128)} %param.14) | copy-start | bytes 28
  78.0 7.9 %all-to-all-start = ((f32[2,4,8,512]{3,2,0,1:T(8,128)}), f32[2,4,8,512]{3,2,0,1:T(8,128)S(1)}, u32[]{:S(2)}, u32[]{:S(2)}) async-start(f32[2,4,8,512]{3,2,0,1:T(8,128)} %copy.14), calls=%async_computation | async-start | bytes 262144 | tf_op jit(solution)/shard_map/all_to_all | solution.py:489

commit v4 on v3

--- a/solution.py
+++ b/solution.py
@@ -181,7 +181,7 @@
 
 
 def compress_kernel(
-    block_cols, counts_ref, phase_ref, echo_ref, turned_ref, band, ready, send_sem, recv_sem,
+    block_cols, counts_ref, phase_ref, rate_ref, echo_ref, turned_ref, filt_ref, band, ready, send_sem, recv_sem,
     own_sem,
 ):
     step = pl.program_id(0)
@@ -273,6 +273,20 @@
 
     @pl.when(step == steps - 1)
     def _():
+        outer, rows, inner = filt_ref.shape[1:]
+        length = outer * inner
+        rate = jnp.pi * rate_ref[...]
+
+        def matched(k, carry):
+            index = k + outer * lax.broadcasted_iota(jnp.int32, (1, inner), 1)
+            signed = jnp.where(index < length // 2, index, index - length).astype(jnp.float32)
+            phase = rate * (signed * signed / length)
+            filt_ref[0, k] = jnp.cos(phase) / length
+            filt_ref[1, k] = -jnp.sin(phase) / length
+            return carry
+
+        lax.fori_loop(0, outer, matched, 0)
+
         def finish(i, carry):
             remote(i // (devices - 1), i % (devices - 1) + 1).wait()
             return carry
@@ -282,9 +296,9 @@
             own(at).wait()
 
 
-def compress_call(echoes, phase, counts, devices):
+def compress_call(echoes, phase, rate, counts, devices, length):
     pulses = echoes.shape[2]
-    step = min(512, pulses)
+    step = min(256, pulses)
     steps = pulses // step
     block_cols = 256
     width = -(-2 * (block_cols + TAPS - 1) // 128) * 128
@@ -292,13 +306,20 @@
     return pl.pallas_call(
         functools.partial(compress_kernel, block_cols),
         grid=(steps,),
-        out_shape=jax.ShapeDtypeStruct((devices, 2, per, pulses), jnp.bfloat16),
+        out_shape=(
+            jax.ShapeDtypeStruct((devices, 2, per, pulses), jnp.bfloat16),
+            jax.ShapeDtypeStruct((2, OUTER, per, length // OUTER), jnp.float32),
+        ),
         in_specs=[
             pl.BlockSpec(memory_space=pltpu.SMEM),
             pl.BlockSpec((1, 2 * TAPS), lambda i: (0, 0)),
+            pl.BlockSpec((per, 1), lambda i: (0, 0)),
             pl.BlockSpec((echoes.shape[0], 2, step), lambda i: (0, 0, i)),
         ],
-        out_specs=pl.BlockSpec(memory_space=pl.ANY),
+        out_specs=(
+            pl.BlockSpec(memory_space=pl.ANY),
+            pl.BlockSpec((2, OUTER, per, length // OUTER), lambda i: (0, 0, 0, 0)),
+        ),
         scratch_shapes=[
             pltpu.VMEM((2, block_cols, width), jnp.bfloat16),
             pltpu.VMEM((steps, devices, 2, per, step), jnp.bfloat16),
@@ -310,7 +331,7 @@
             vmem_limit_bytes=40 * 2**20, collective_id=0, has_side_effects=True
         ),
         name="compress",
-    )(counts, phase, echoes)
+    )(counts, phase, rate, echoes)
 
 
 def focus_kernel(
@@ -438,18 +459,6 @@
     return pairs, twist, fwd, inv, pool, look
 
 
-def matched_filter(rate, length):
-    inner = length // OUTER
-    index = (
-        jnp.arange(OUTER, dtype=jnp.int32)[:, None]
-        + OUTER * jnp.arange(inner, dtype=jnp.int32)[None, :]
-    )
-    signed = jnp.where(index < length // 2, index, index - length).astype(jnp.float32)
-    quad = signed * signed / length
-    phase = (jnp.pi * rate)[None, :, None] * quad[:, None, :]
-    return jnp.stack([jnp.cos(phase), -jnp.sin(phase)]) / length
-
-
 def focus_call(x, filt, acqs):
     rows, local = x.shape[2], x.shape[3]
     length = x.shape[0] // acqs * local
@@ -480,9 +489,11 @@
     looks = rows // LOOK_RNG
     first = lax.axis_index("pulse") * pulses_dev
     counts = jnp.stack([pulse_counts[0], first.astype(jnp.int32)])
-    x = compress_call(echoes, jnp.repeat(chirp_phase, 2)[None], counts, acqs * turns)
     rate = lax.dynamic_slice(azimuth_rate, (lax.axis_index("acq") * rows,), (rows,))
-    filt = matched_filter(rate, pulses_dev * turns)
+    x, filt = compress_call(
+        echoes, jnp.repeat(chirp_phase, 2)[None], rate[:, None], counts, acqs * turns,
+        pulses_dev * turns,
+    )
     out = focus_call(x, filt, acqs)
     cells = out.shape[2]
     out = out.reshape(2, acqs, bits * looks, cells)

time: 87.7 us -> 86.8 us (0.990)
  other arithmetic: 4.13 us -> 1.36 us
  Pallas kernels: 69.1 us -> 70.2 us
    cos x1 -> x0, other arithmetic: 1.91 us -> none  [matched_filter(): return jnp.stack([jnp.cos(phase), -jnp.sin(phase)]) / length]
    pallas_call x1, Pallas kernels: 56.3 us -> 57.4 us  [compress_call(): pl.pallas_call(functools.partial(compress_kernel, block_cols), grid=(step...]
    unnamed x12 -> x14, local copies, waits for them, and re-layouts: 2.8 us -> 3.45 us
where the time goes in v4:
time: 86.8 us; the launch traced here: 86.5 us
  Pallas kernels  70.2 us (81%)
  local copies, waits for them, and re-layouts  6.16 us (7%)
  starting transfers between devices  3.32 us (4%)
  between operations  2.72 us (3%)
  waiting for transfers between devices  2.7 us (3%)
  other arithmetic  1.36 us (2%)
    pallas_call x1, Pallas kernels, compress_call(): pl.pallas_call(functools.partial(compress_kernel, block_cols), grid=(step...  57.4 us
    pallas_call x1, Pallas kernels, focus_call(): pl.pallas_call(functools.partial(focus_kernel, acqs, pairs), out_shape=ja...  12.8 us
    unnamed x14, local copies, waits for them, and re-layouts  3.45 us
    all_to_all x1, starting transfers between devices, per_device_joint(): out = lax.all_to_all(out, 'acq', split_axis=1, concat_axis=1, tiled=True)  3.32 us
    all_to_all x1, waiting for transfers between devices, per_device_joint(): out = lax.all_to_all(out, 'acq', split_axis=1, concat_axis=1, tiled=True)  2.7 us
  transfers between devices with their start and end apart: 1, of which 1 were waited for; matrix products, arithmetic and copies ran while one was open for 1% of the time, Pallas kernels for 0%

profile of v4, /device:TPU:0, one launch (start us, length us, event | category | flops | bytes accessed | tf_op | source)
XLA Modules:
  0.0 86.5 jit_solution(17305766361079641274)
XLA Ops:
  0.6 0.0 copy-start
  0.7 0.6 copy-done
  1.3 0.1 dynamic-slice_bitcast_fusion
  1.4 0.1 copy.16.rate_ref
  2.1 0.9 %broadcast_in_dim.12 = f32[1024,2]{1,0:T(8,128)S(1)} broadcast(f32[1024]{0:T(1024)} %param.11), dimensions={0} | broadcast | bytes 12288 | tf_op jit(solution)/shard_map/broadcast_in_dim | solution.py:494
  3.0 0.3 broadcast_in_dim_reshape.3.phase_ref
  3.3 0.1 pad_add_fusion.counts_ref
  3.4 0.0 copy-start.1
  3.4 2.8 %copy-done.1 = bf16[1,2,1024,1535]{2,1,3,0:T(2,128)(2,1)S(1)} copy-done((bf16[1,2,1024,1535]{2,1,3,0:T(2,128)(2,1)S(1)}, bf16[1,2,1024,1535]{2,1,3,0:T(2,128)(2,1)}, u32[]{:S(2)}) %copy-start.1) | copy-done | bytes 6287384
  6.2 0.0 copy-start.2
  6.2 0.0 copy-start.3
  6.2 0.0 copy-start.4
  6.2 0.0 copy-start.5
  6.2 57.4 %compress.1 = (bf16[32,2,16,1024]{3,2,1,0:T(8,128)(2,1)S(1)}, f32[2,16,16,512]{3,2,1,0:T(8,128)S(1)}) custom-call(s32[2]{0:T(128)S(1)} %pad_add_fusion.counts_ref, f32[1,2048]{1,0:T(1,128)S(1)} %broadcast_in_dim_reshape.3.phase_ref, f32[16,1]{1,0:T(8,128)S(1)} %copy.16.rate_ref, bf16[1535,2,1024]{2,1,0:T(2,128)(2,1)S(1)} %bitcast.26), custom_call_target="tpu_custom_call" | custom-call | tf_op jit(solution)/shard_map/compress/pallas_call | solution.py:306
  63.6 0.0 copy-done.2
  63.6 0.0 copy-done.3
  63.6 0.0 copy-done.4
  63.7 0.0 copy-done.5
  63.7 0.0 copy-start.6
  63.7 12.8 %focus.1 = f32[2,32,512]{2,1,0:T(8,128)S(1)} custom-call(bf16[32,2,16,1024]{3,2,1,0:T(8,128)(2,1)S(1)} %get-tuple-element.4.x_ref, f32[2,16,16,512]{3,2,1,0:T(8,128)S(1)} %get-tuple-element.5.filt_ref, f32[2,16,512]{2,1,0:T(8,128)S(1)} %copy-done.4, bf16[1024,1024]{1,0:T(8,128)(2,1)S(1)} %copy-done.2, bf16[1024,1024]{1,0:T(8,128)(2,1)} %constant.32.clone.inv_ref, ...), custom_call_target="tpu_custom_call" | custom-call | tf_op jit(solution)/shard_map/focus/pallas_call | solution.py:467
  76.5 0.7 copy.17
  77.1 3.3 %all-to-all-start = ((f32[2,4,8,512]{3,2,0,1:T(8,128)}), f32[2,4,8,512]{3,2,0,1:T(8,128)S(1)}, u32[]{:S(2)}, u32[]{:S(2)}) async-start(f32[2,4,8,512]{3,2,0,1:T(8,128)} %copy.17), calls=%async_computation | async-start | bytes 262144 | tf_op jit(solution)/shard_map/all_to_all | solution.py:500
  80.5 0.0 copy-done.6
  80.5 0.6 fusion
  82.3 2.7 %all-to-all-done = f32[2,4,8,512]{3,2,0,1:T(8,128)S(1)} async-done(((f32[2,4,8,512]{3,2,0,1:T(8,128)}), f32[2,4,8,512]{3,2,0,1:T(8,128)S(1)}, u32[]{:S(2)}, u32[]{:S(2)}) %all-to-all-start) | async-done | bytes 131104 | tf_op jit(solution)/shard_map/all_to_all | solution.py:500
  85.2 0.6 maximum_bitcast_fusion.1
  85.8 0.6 maximum_bitcast_fusion
  (5 shorter events, 0.1 us)
Async XLA Ops:
  0.6 0.7 copy-start
  3.4 2.8 %copy-start.1 = (bf16[1,2,1024,1535]{2,1,3,0:T(2,128)(2,1)S(1)}, bf16[1,2,1024,1535]{2,1,3,0:T(2,128)(2,1)}, u32[]{:S(2)}) copy-start(bf16[1,2,1024,1535]{2,1,3,0:T(2,128)(2,1)} %param.10) | copy-start | bytes 18862084
  6.2 57.5 %copy-start.2 = (bf16[1024,1024]{1,0:T(8,128)(2,1)S(1)}, bf16[1024,1024]{1,0:T(8,128)(2,1)}, u32[]{:S(2)}) copy-start(bf16[1024,1024]{1,0:T(8,128)(2,1)} %constant.31.clone.fwd_ref) | copy-start | bytes 6291460
  6.2 57.5 %copy-start.3 = (bf16[2048,128]{1,0:T(8,128)(2,1)S(1)}, bf16[2048,128]{1,0:T(8,128)(2,1)}, u32[]{:S(2)}) copy-start(bf16[2048,128]{1,0:T(8,128)(2,1)} %constant.33.clone.pool_ref) | copy-start | bytes 1572868
  6.2 57.5 %copy-start.4 = (f32[2,16,512]{2,1,0:T(8,128)S(1)}, f32[2,16,512]{2,1,0:T(8,128)}, u32[]{:S(2)}) copy-start(f32[2,16,512]{2,1,0:T(8,128)} %constant.30.clone.twist_ref) | copy-start | bytes 196612
  6.2 57.5 %copy-start.5 = (f32[2,32,64]{2,1,0:T(8,128)S(1)}, f32[2,32,64]{2,1,0:T(8,128)}, u32[]{:S(2)}) copy-start(f32[2,32,64]{2,1,0:T(8,128)} %constant.34.clone.look_ref) | copy-start | bytes 49156
  63.7 16.8 %copy-start.6 = (s32[1,2]{1,0:T(1,128)S(1)}, s32[1,2]{1,0:T(1,128)}, u32[]{:S(2)}) copy-start(s32[1,2]{1,0:T(1,128)} %param.14) | copy-start | bytes 28
  77.1 7.9 %all-to-all-start = ((f32[2,4,8,512]{3,2,0,1:T(8,128)}), f32[2,4,8,512]{3,2,0,1:T(8,128)S(1)}, u32[]{:S(2)}, u32[]{:S(2)}) async-start(f32[2,4,8,512]{3,2,0,1:T(8,128)} %copy.17), calls=%async_computation | async-start | bytes 262144 | tf_op jit(solution)/shard_map/all_to_all | solution.py:500

commit v5 on v4

--- a/solution.py
+++ b/solution.py
@@ -335,9 +335,16 @@
 
 
 def focus_kernel(
-    acqs, pairs, x_ref, filt_ref, twist_ref, fwd_ref, inv_ref, pool_ref, look_ref, out_ref,
-    held, image, prods,
+    acqs, pairs, chosen_ref, x_ref, filt_ref, twist_ref, fwd_ref, inv_ref, pool_ref, look_ref,
+    real_ref, imag_ref, held, image, prods, stage, landed, send_sem, recv_sem, own_sem,
 ):
+    me = lax.axis_index("acq")
+    pulse = lax.axis_index("pulse")
+    barrier = pltpu.get_barrier_semaphore()
+    for d in range(1, acqs):
+        pl.semaphore_signal(
+            barrier, inc=1, device_id=(me ^ d, pulse), device_id_type=pl.DeviceIdType.MESH
+        )
     rows = x_ref.shape[2]
     local = x_ref.shape[3]
     inner = twist_ref.shape[2]
@@ -426,10 +433,43 @@
         parts[0].append(z[:count])
         parts[1].append(z[count:])
     for part in range(2):
-        out_ref[part] = jnp.dot(
+        result = jnp.dot(
             look_ref[part], jnp.concatenate(parts[part], axis=1),
             preferred_element_type=jnp.float32, precision=lax.Precision.HIGHEST,
         )
+        span = result.shape[0] // acqs
+        for acq in range(acqs):
+            stage[acq, part] = result[acq * span : (acq + 1) * span]
+
+    pl.semaphore_wait(barrier, acqs - 1)
+    copies = [
+        pltpu.make_async_remote_copy(
+            src_ref=stage.at[me ^ d], dst_ref=landed.at[me],
+            send_sem=send_sem.at[d], recv_sem=recv_sem.at[d],
+            device_id=(me ^ d, pulse), device_id_type=pl.DeviceIdType.MESH,
+        )
+        for d in range(1, acqs)
+    ]
+    copies.append(pltpu.make_async_copy(stage.at[me], landed.at[me], own_sem))
+    for copy in copies:
+        copy.start()
+    for copy in copies:
+        copy.wait()
+    bits = acqs.bit_length() - 1
+    looks = rows // LOOK_RNG
+    for part, ref in enumerate((real_ref, imag_ref)):
+        for slot in range(2):
+            bit = chosen_ref[slot]
+            blocks = []
+            for src in range(acqs):
+                block = landed[src, part]
+                taken = block[:looks]
+                for which in range(1, bits):
+                    taken = jnp.where(
+                        bit == which, block[which * looks : (which + 1) * looks], taken
+                    )
+                blocks.append(taken)
+            ref[slot] = jnp.concatenate(blocks, axis=0)
 
 
 def focus_tables(acqs, rows, length):
@@ -459,24 +499,34 @@
     return pairs, twist, fwd, inv, pool, look
 
 
-def focus_call(x, filt, acqs):
+def focus_call(x, filt, chosen, acqs):
     rows, local = x.shape[2], x.shape[3]
     length = x.shape[0] // acqs * local
     inner = length // OUTER
     pairs, twist, fwd, inv, pool, look = focus_tables(acqs, rows, length)
     return pl.pallas_call(
         functools.partial(focus_kernel, acqs, pairs),
-        out_shape=jax.ShapeDtypeStruct((2, look.shape[1], length // LOOK_AZ), jnp.float32),
-        in_specs=[pl.BlockSpec(memory_space=pltpu.VMEM)] * 7,
-        out_specs=pl.BlockSpec(memory_space=pltpu.VMEM),
+        out_shape=(
+            jax.ShapeDtypeStruct((2, acqs * rows // LOOK_RNG, length // LOOK_AZ), jnp.float32),
+        ) * 2,
+        in_specs=[pl.BlockSpec(memory_space=pltpu.SMEM)]
+        + [pl.BlockSpec(memory_space=pltpu.VMEM)] * 7,
+        out_specs=(pl.BlockSpec(memory_space=pltpu.VMEM),) * 2,
         scratch_shapes=[
             pltpu.VMEM((acqs, OUTER, rows, 2 * inner), jnp.bfloat16),
             pltpu.VMEM((acqs, OUTER, rows, 2 * inner), jnp.float32),
             pltpu.VMEM((4 * len(pairs) * rows, pool.shape[0]), jnp.bfloat16),
+            pltpu.VMEM((acqs, 2, look.shape[1] // acqs, length // LOOK_AZ), jnp.float32),
+            pltpu.VMEM((acqs, 2, look.shape[1] // acqs, length // LOOK_AZ), jnp.float32),
+            pltpu.SemaphoreType.DMA((acqs,)),
+            pltpu.SemaphoreType.DMA((acqs,)),
+            pltpu.SemaphoreType.DMA,
         ],
-        compiler_params=pltpu.CompilerParams(vmem_limit_bytes=48 * 2**20),
+        compiler_params=pltpu.CompilerParams(
+            vmem_limit_bytes=48 * 2**20, collective_id=1, has_side_effects=True
+        ),
         name="focus",
-    )(x, filt, jnp.asarray(twist), jnp.asarray(fwd), jnp.asarray(inv), jnp.asarray(pool),
+    )(chosen, x, filt, jnp.asarray(twist), jnp.asarray(fwd), jnp.asarray(inv), jnp.asarray(pool),
       jnp.asarray(look))
 
 
@@ -484,9 +534,7 @@
     echoes = raw_echo[0].transpose(2, 0, 1)
     pulses_dev = echoes.shape[2]
     acqs, turns = lax.axis_size("acq"), lax.axis_size("pulse")
-    bits = acqs.bit_length() - 1
     rows = RNG // (acqs * turns)
-    looks = rows // LOOK_RNG
     first = lax.axis_index("pulse") * pulses_dev
     counts = jnp.stack([pulse_counts[0], first.astype(jnp.int32)])
     rate = lax.dynamic_slice(azimuth_rate, (lax.axis_index("acq") * rows,), (rows,))
@@ -494,23 +542,8 @@
         echoes, jnp.repeat(chirp_phase, 2)[None], rate[:, None], counts, acqs * turns,
         pulses_dev * turns,
     )
-    out = focus_call(x, filt, acqs)
-    cells = out.shape[2]
-    out = out.reshape(2, acqs, bits * looks, cells)
-    out = lax.all_to_all(out, "acq", split_axis=1, concat_axis=1, tiled=True)
-    out = out.reshape(2, acqs, bits, looks, cells).transpose(0, 2, 1, 3, 4)
-    out = out.reshape(2, bits, acqs * looks, cells)
-    chosen = partner_bits[0]
-    slots = []
-    for slot in range(2):
-        taken = out[:, 0]
-        for which in range(1, bits):
-            taken = jnp.where(chosen[slot] == which, out[:, which], taken)
-        slots.append(taken)
-    return (
-        jnp.stack([item[0] for item in slots])[None],
-        jnp.stack([item[1] for item in slots])[None],
-    )
+    real, imag = focus_call(x, filt, partner_bits[0], acqs)
+    return (real[None], imag[None])
 
 
 def solution(mesh):

time: 86.8 us -> 80.4 us (0.926)
  starting transfers between devices: 3.32 us -> 0 us
  Pallas kernels: 70.2 us -> 73.3 us
  waiting for transfers between devices: 2.7 us -> 0 us
  between operations: 2.72 us -> 1.39 us
  other arithmetic: 1.36 us -> 0.08 us
    all_to_all x1 -> x0, starting transfers between devices: 3.32 us -> none  [per_device_joint(): out = lax.all_to_all(out, 'acq', split_axis=1, concat_axis=1, tiled=True)]
    pallas_call x1, Pallas kernels: 12.8 us -> 15.9 us  [focus_call(): pl.pallas_call(functools.partial(focus_kernel, acqs, pairs), out_shape=(j...]
    all_to_all x1 -> x0, waiting for transfers between devices: 2.7 us -> none  [per_device_joint(): out = lax.all_to_all(out, 'acq', split_axis=1, concat_axis=1, tiled=True)]
    broadcast_in_dim x2 -> x0, other arithmetic: 1.27 us -> none  [the longest x1 0.64 us: per_device_joint(): jnp.stack([item[1] for item in slots])[None]]
    unnamed x14 -> x16, local copies, waits for them, and re-layouts: 3.45 us -> 4.07 us
  transfers between devices with their start and end apart: 1 -> 0, of which waited for: 1 -> 0; matrix products, arithmetic and copies ran while one was open for 1% -> 0% of each run, Pallas kernels for 0% -> 0%
where the time goes in v5:
time: 80.4 us; the launch traced here: 80.2 us
  Pallas kernels  73.3 us (91%)
  local copies, waits for them, and re-layouts  5.42 us (7%)
  between operations  1.39 us (2%)
    pallas_call x1, Pallas kernels, compress_call(): pl.pallas_call(functools.partial(compress_kernel, block_cols), grid=(step...  57.4 us
    pallas_call x1, Pallas kernels, focus_call(): pl.pallas_call(functools.partial(focus_kernel, acqs, pairs), out_shape=(j...  15.9 us
    unnamed x16, local copies, waits for them, and re-layouts  4.07 us

profile of v5, /device:TPU:0, one launch (start us, length us, event | category | flops | bytes accessed | tf_op | source)
XLA Modules:
  0.0 80.2 jit_solution(3154065846278263836)
XLA Ops:
  0.6 0.0 copy-start
  1.3 0.1 pad_add_fusion.counts_ref
  1.4 0.0 copy-done
  1.4 0.1 dynamic-slice_bitcast_fusion
  1.5 0.1 copy.13.rate_ref
  1.5 0.9 %broadcast_in_dim.12 = f32[1024,2]{1,0:T(8,128)S(1)} broadcast(f32[1024]{0:T(1024)} %param.11), dimensions={0} | broadcast | bytes 12288 | tf_op jit(solution)/shard_map/broadcast_in_dim | solution.py:542
  2.4 0.3 broadcast_in_dim_reshape.3.phase_ref
  2.7 0.0 copy-start.1
  2.8 2.8 %copy-done.1 = bf16[1,2,1024,1535]{2,1,3,0:T(2,128)(2,1)S(1)} copy-done((bf16[1,2,1024,1535]{2,1,3,0:T(2,128)(2,1)S(1)}, bf16[1,2,1024,1535]{2,1,3,0:T(2,128)(2,1)}, u32[]{:S(2)}) %copy-start.1) | copy-done | bytes 6287384
  5.5 0.0 copy-start.2
  5.5 0.0 copy-start.3
  5.5 0.0 copy-start.4
  5.5 0.0 copy-start.5
  5.5 0.0 copy-start.6
  5.6 57.4 %compress.1 = (bf16[32,2,16,1024]{3,2,1,0:T(8,128)(2,1)S(1)}, f32[2,16,16,512]{3,2,1,0:T(8,128)S(1)}) custom-call(s32[2]{0:T(128)S(1)} %pad_add_fusion.counts_ref, f32[1,2048]{1,0:T(1,128)S(1)} %broadcast_in_dim_reshape.3.phase_ref, f32[16,1]{1,0:T(8,128)S(1)} %copy.13.rate_ref, bf16[1535,2,1024]{2,1,0:T(2,128)(2,1)S(1)} %bitcast.9), custom_call_target="tpu_custom_call" | custom-call | tf_op jit(solution)/shard_map/compress/pallas_call | solution.py:306
  63.0 0.0 copy-done.2
  63.0 0.0 copy-done.3
  63.0 0.0 copy-done.4
  63.0 0.0 copy-done.5
  63.0 0.0 copy-done.6
  63.1 15.9 %focus.1 = (f32[2,16,512]{2,1,0:T(8,128)S(1)}, f32[2,16,512]{2,1,0:T(8,128)S(1)}) custom-call(s32[2]{0:T(128)S(1)} %bitcast.12, bf16[32,2,16,1024]{3,2,1,0:T(8,128)(2,1)S(1)} %get-tuple-element.6.x_ref, f32[2,16,16,512]{3,2,1,0:T(8,128)S(1)} %get-tuple-element.7.filt_ref, f32[2,16,512]{2,1,0:T(8,128)S(1)} %copy-done.4, bf16[1024,1024]{1,0:T(8,128)(2,1)S(1)} %copy-done.2, ...), custom_call_target="tpu_custom_call" | custom-call | tf_op jit(solution)/shard_map/focus/pallas_call | solution.py:507
  78.9 0.6 copy.17
  79.5 0.6 copy.18
Async XLA Ops:
  0.6 0.8 copy-start
  2.7 2.8 %copy-start.1 = (bf16[1,2,1024,1535]{2,1,3,0:T(2,128)(2,1)S(1)}, bf16[1,2,1024,1535]{2,1,3,0:T(2,128)(2,1)}, u32[]{:S(2)}) copy-start(bf16[1,2,1024,1535]{2,1,3,0:T(2,128)(2,1)} %param.10) | copy-start | bytes 18862084
  5.5 57.5 %copy-start.2 = (bf16[1024,1024]{1,0:T(8,128)(2,1)S(1)}, bf16[1024,1024]{1,0:T(8,128)(2,1)}, u32[]{:S(2)}) copy-start(bf16[1024,1024]{1,0:T(8,128)(2,1)} %constant.27.clone.fwd_ref) | copy-start | bytes 6291460
  5.5 57.5 %copy-start.3 = (bf16[2048,128]{1,0:T(8,128)(2,1)S(1)}, bf16[2048,128]{1,0:T(8,128)(2,1)}, u32[]{:S(2)}) copy-start(bf16[2048,128]{1,0:T(8,128)(2,1)} %constant.29.clone.pool_ref) | copy-start | bytes 1572868
  5.5 57.5 %copy-start.4 = (f32[2,16,512]{2,1,0:T(8,128)S(1)}, f32[2,16,512]{2,1,0:T(8,128)}, u32[]{:S(2)}) copy-start(f32[2,16,512]{2,1,0:T(8,128)} %constant.26.clone.twist_ref) | copy-start | bytes 196612
  5.5 57.5 %copy-start.5 = (f32[2,32,64]{2,1,0:T(8,128)S(1)}, f32[2,32,64]{2,1,0:T(8,128)}, u32[]{:S(2)}) copy-start(f32[2,32,64]{2,1,0:T(8,128)} %constant.30.clone.look_ref) | copy-start | bytes 49156
  5.5 57.5 %copy-start.6 = (s32[1,2]{1,0:T(1,128)S(1)}, s32[1,2]{1,0:T(1,128)}, u32[]{:S(2)}) copy-start(s32[1,2]{1,0:T(1,128)} %param.14) | copy-start | bytes 28

commit v6 on v5

--- a/solution.py
+++ b/solution.py
@@ -328,7 +328,7 @@
             pltpu.SemaphoreType.DMA((steps,)),
         ],
         compiler_params=pltpu.CompilerParams(
-            vmem_limit_bytes=40 * 2**20, collective_id=0, has_side_effects=True
+            vmem_limit_bytes=49 * 2**20, collective_id=0, has_side_effects=True
         ),
         name="compress",
     )(counts, phase, rate, echoes)

time: 80.4 us -> 78.3 us (0.974)
  local copies, waits for them, and re-layouts: 5.42 us -> 2.66 us
    unnamed x16 -> x14, local copies, waits for them, and re-layouts: 4.07 us -> 1.3 us
where the time goes in v6:
time: 78.3 us; the launch traced here: 78.1 us
  Pallas kernels  74 us (95%)
  local copies, waits for them, and re-layouts  2.66 us (3%)
  between operations  1.41 us (2%)
    pallas_call x1, Pallas kernels, compress_call(): pl.pallas_call(functools.partial(compress_kernel, block_cols), grid=(step...  57.9 us
    pallas_call x1, Pallas kernels, focus_call(): pl.pallas_call(functools.partial(focus_kernel, acqs, pairs), out_shape=(j...  16.1 us

profile of v6, /device:TPU:0, one launch (start us, length us, event | category | flops | bytes accessed | tf_op | source)
XLA Modules:
  0.0 78.1 jit_solution(11989877231213767907)
XLA Ops:
  0.6 0.0 copy-start
  1.3 0.1 pad_add_fusion.counts_ref
  1.4 0.0 copy-done
  1.4 0.1 dynamic-slice_bitcast_fusion
  1.5 0.1 copy.13.rate_ref
  1.5 0.9 %broadcast_in_dim.12 = f32[1024,2]{1,0:T(8,128)S(1)} broadcast(f32[1024]{0:T(1024)} %param.11), dimensions={0} | broadcast | bytes 12288 | tf_op jit(solution)/shard_map/broadcast_in_dim | solution.py:542
  2.4 0.3 broadcast_in_dim_reshape.3.phase_ref
  2.7 0.0 copy-start.1
  2.8 0.0 copy-start.2
  2.8 0.0 copy-start.3
  2.8 0.0 copy-start.4
  2.8 0.0 copy-start.5
  2.8 57.9 %compress.1 = (bf16[32,2,16,1024]{3,2,1,0:T(8,128)(2,1)S(1)}, f32[2,16,16,512]{3,2,1,0:T(8,128)S(1)}) custom-call(s32[2]{0:T(128)S(1)} %pad_add_fusion.counts_ref, f32[1,2048]{1,0:T(1,128)S(1)} %broadcast_in_dim_reshape.3.phase_ref, f32[16,1]{1,0:T(8,128)S(1)} %copy.13.rate_ref, bf16[1535,2,1024]{2,1,0:T(2,128)(2,1)} %bitcast.12), custom_call_target="tpu_custom_call" | custom-call | tf_op jit(solution)/shard_map/compress/pallas_call | solution.py:306
  60.7 0.0 copy-done.1
  60.7 0.0 copy-done.2
  60.7 0.0 copy-done.3
  60.7 0.0 copy-done.4
  60.7 0.0 copy-done.5
  60.8 16.1 %focus.1 = (f32[2,16,512]{2,1,0:T(8,128)S(1)}, f32[2,16,512]{2,1,0:T(8,128)S(1)}) custom-call(s32[2]{0:T(128)S(1)} %bitcast.11, bf16[32,2,16,1024]{3,2,1,0:T(8,128)(2,1)S(1)} %get-tuple-element.6.x_ref, f32[2,16,16,512]{3,2,1,0:T(8,128)S(1)} %get-tuple-element.7.filt_ref, f32[2,16,512]{2,1,0:T(8,128)S(1)} %copy-done.3, bf16[1024,1024]{1,0:T(8,128)(2,1)S(1)} %copy-done.1, ...), custom_call_target="tpu_custom_call" | custom-call | tf_op jit(solution)/shard_map/focus/pallas_call | solution.py:507
  76.8 0.6 copy.17
  77.5 0.6 copy.18
Async XLA Ops:
  0.6 0.8 copy-start
  2.7 58.0 %copy-start.1 = (bf16[1024,1024]{1,0:T(8,128)(2,1)S(1)}, bf16[1024,1024]{1,0:T(8,128)(2,1)}, u32[]{:S(2)}) copy-start(bf16[1024,1024]{1,0:T(8,128)(2,1)} %constant.27.clone.fwd_ref) | copy-start | bytes 6291460
  2.8 58.0 %copy-start.2 = (bf16[2048,128]{1,0:T(8,128)(2,1)S(1)}, bf16[2048,128]{1,0:T(8,128)(2,1)}, u32[]{:S(2)}) copy-start(bf16[2048,128]{1,0:T(8,128)(2,1)} %constant.29.clone.pool_ref) | copy-start | bytes 1572868
  2.8 58.0 %copy-start.3 = (f32[2,16,512]{2,1,0:T(8,128)S(1)}, f32[2,16,512]{2,1,0:T(8,128)}, u32[]{:S(2)}) copy-start(f32[2,16,512]{2,1,0:T(8,128)} %constant.26.clone.twist_ref) | copy-start | bytes 196612
  2.8 57.9 %copy-start.4 = (f32[2,32,64]{2,1,0:T(8,128)S(1)}, f32[2,32,64]{2,1,0:T(8,128)}, u32[]{:S(2)}) copy-start(f32[2,32,64]{2,1,0:T(8,128)} %constant.30.clone.look_ref) | copy-start | bytes 49156
  2.8 57.9 %copy-start.5 = (s32[1,2]{1,0:T(1,128)S(1)}, s32[1,2]{1,0:T(1,128)}, u32[]{:S(2)}) copy-start(s32[1,2]{1,0:T(1,128)} %param.14) | copy-start | bytes 28
